TPU v7x, 512 devices: a whole 4x8x8 slice. The times are simulated.
512 devices in a mesh: snap: 16 (over y_lo, x, core), space: 32 (over z, y_hi).
Axes of the slice: x: 4, y: 8 (y_hi: 4, y_lo: 2; y = y_hi * 2 + y_lo), z: 8, core: 2. Of those that a mesh axis runs over, the one named last changes fastest.
Arguments:
- snapshots: bfloat16 [32768, 2048], P('space', 'snap')
- cell_weight: float32 [32768], P('space'), may hold values from 0.2 to 2
- eigvec: bfloat16 [2048, 256], replicated, may hold values from -0.125 to 0.125
- time_index: int32 [2048], replicated, may hold values from 0 to 2047, each once
Outputs:
- gram: float32 [2048, 2048], P('space', 'snap')
- modes: float32 [256, 32768], P('snap', 'space')
Inputs may be any that keep to these rules, and one draw needn't show every extreme that they name: `time_index`: each value of 0 to 2047 appears exactly once.
All inputs are finite; a program needn't handle non-finite values.
Results may differ from a plain program's by a relative error of at most 0.00081.
Values may be sent and summed in bfloat16 or wider, within the bound.
No kernel may reach another device: no remote copies, remote signals or barrier semaphores. Data moves between devices by JAX's collectives and lax.ppermute only.
A program may use at most 64 MiB of HBM per device.

v0:
```python
import jax
import jax.numpy as jnp
from jax import lax
from jax.sharding import PartitionSpec as P


def contract_rows(left, right):
    return lax.dot_general(
        left, right, (((0,), (0,)), ((), ())), preferred_element_type=jnp.float32
    )


def reduce_gram(make_rows, share_rows):
    return lax.psum_scatter(
        make_rows(jnp.int32(0), lax.axis_size("space") * share_rows),
        "space",
        scatter_dimension=0,
        tiled=True,
    )


def body(snapshots, cell_weight, eigvec, time_index):
    row_count, block_size = snapshots.shape
    snap_count = lax.axis_size("snap")
    snapshot_total = block_size * snap_count
    gram_share = snapshot_total // lax.axis_size("space")
    scaling = 1.0 / (row_count * lax.axis_size("space"))
    weighted = (snapshots.astype(jnp.float32) * cell_weight[:, None]).astype(jnp.bfloat16)
    ordered = jnp.take(eigvec, time_index, axis=0)
    mode_part = None
    gathered = lax.all_gather(snapshots, "snap", axis=1, tiled=True)

    def gram_terms(offset, length):
        return contract_rows(gathered, weighted) * scaling

    gram = reduce_gram(gram_terms, gram_share)
    local_weights = lax.dynamic_slice_in_dim(
        ordered, lax.axis_index("snap") * block_size, block_size, 0
    )
    mode_part = lax.psum_scatter(
        lax.dot_general(
            local_weights, snapshots, (((0,), (1,)), ((), ())), preferred_element_type=jnp.float32
        ),
        "snap",
        scatter_dimension=0,
        tiled=True,
    )
    return (gram, mode_part)


def solution(mesh):
    in_specs = (P("space", "snap"), P("space"), P(), P())
    out_specs = (P("space", "snap"), P("snap", "space"))
    return jax.shard_map(body, mesh=mesh, in_specs=in_specs, out_specs=out_specs, check_vma=False)
```

profile of v0, /device:TPU:6, one launch (start us, length us, event | category | flops | bytes accessed | tf_op | source)
XLA Modules:
  0.0 370.8 jit_solution(7543757270800126859)
XLA Ops:
  7.2 0.0 copy-start
  7.2 0.0 all-gather.2.cloned.1.call-start
  7.2 0.7 all-gather.2.cloned.1.call-update
  7.9 0.0 reduce-scatter.5.cloned.1.call-start
  8.0 0.7 fusion.5
  8.7 0.0 copy-done
  8.7 0.0 copy-start.2
  8.7 0.0 copy-start.1
  8.7 0.0 copy-start.3
  8.7 7.5 %gather_fusion = bf16[2048,256]{1,0:T(8,128)(2,1)S(1)} fusion(bf16[2048,256]{1,0:T(8,128)(2,1)S(1)} %copy-done, s32[2048]{0:T(1024)S(1)} %fusion.5), kind=kCustom, calls=%fused_computation | custom fusion | bytes 2105344 | tf_op jit(solution)/shard_map/jit(_take)/gather | solution.py:29
  16.2 0.0 copy-done.2
  16.2 0.1 dynamic-slice
  16.3 0.0 copy-done.1
  16.3 1.4 fusion.2
  17.7 0.0 reduce-scatter.5.cloned.1.call-update
  17.7 0.0 reduce-scatter.7.cloned.1.call-start
  17.8 46.7 %all-gather.2.cloned.1.call-done = bf16[1024,2048]{1,0:T(8,128)(2,1)} async-done(((bf16[1024,128]{1,0:T(8,128)(2,1)}), bf16[1024,2048]{1,0:T(8,128)(2,1)}) %all-gather.2.cloned.1.call-update) | async-done | bytes 4194320 | tf_op jit(solution)/shard_map/all_gather | solution.py:31
  64.4 0.0 copy-done.3
  64.4 3.0 fusion
  67.5 1.3 copy.8
  68.8 0.0 reduce-scatter.7.cloned.1.call-update
  68.8 62.5 %reduce-scatter.5.cloned.1.call-done = f32[16,1024]{1,0:T(8,128)} async-done(((f32[256,1024]{1,0:T(8,128)}), f32[16,1024]{1,0:T(8,128)}) %reduce-scatter.5.cloned.1.call-update) | async-done | bytes 65552 | tf_op jit(solution)/shard_map/reduce_scatter | solution.py:40
  131.3 232.9 %reduce-scatter.7.cloned.1.call-done = f32[64,128]{1,0:T(8,128)} async-done(((f32[2048,128]{1,0:T(8,128)}), f32[64,128]{1,0:T(8,128)}) %reduce-scatter.7.cloned.1.call-update) | async-done | bytes 32784
  (1 shorter events, 0.0 us)
Async XLA Ops:
  7.2 1.5 copy-start
  7.2 57.3 %all-gather.2.cloned.1.call-start = ((), (), s32[]{:S(2)}) async-start(), calls=%async_computation.2 | async-start | bytes 4456448 | tf_op jit(solution)/shard_map/all_gather | solution.py:31
  7.9 123.4 %reduce-scatter.5.cloned.1.call-start = ((), (), s32[]{:S(2)}) async-start(), calls=%async_computation.3 | async-start | bytes 1114112 | tf_op jit(solution)/shard_map/reduce_scatter | solution.py:40
  8.7 7.5 %copy-start.2 = (s32[2048]{0:T(1024)S(1)}, s32[2048]{0:T(1024)}, u32[]{:S(2)}) copy-start(s32[2048]{0:T(1024)} %param.7) | copy-start | bytes 24580
  8.7 7.6 %copy-start.1 = (bf16[1024,128]{1,0:T(8,128)(2,1)S(1)}, bf16[1024,128]{1,0:T(8,128)(2,1)}, u32[]{:S(2)}) copy-start(bf16[1024,128]{1,0:T(8,128)(2,1)} %param.4) | copy-start | bytes 786436
  8.7 55.8 %copy-start.3 = (f32[1024]{0:T(1024)S(1)}, f32[1024]{0:T(1024)}, u32[]{:S(2)}) copy-start(f32[1024]{0:T(1024)} %param.5) | copy-start | bytes 12292
  17.7 346.5 %reduce-scatter.7.cloned.1.call-start = ((), (), s32[]{:S(2)}) async-start(), calls=%async_computation.4 | async-start | bytes 1081344
Sparse Core Ops, SparseCore 0:
  10.1 54.3 all-gather.1
  67.8 63.4 reduce-scatter.4
  136.9 227.2 reduce-scatter.6
where the time goes:
time: 371 us
  waiting for transfers between devices  343 us (92%)
  between operations  13.8 us (4%)
  local copies, waits for them, and re-layouts  8.91 us (2%)
  matrix products  4.38 us (1%)
    unnamed x4, waiting for transfers between devices  234 us
    reduce_scatter x1, waiting for transfers between devices, body(): lax.psum_scatter(lax.dot_general(local_weights, snapshots, (((0,), (1,)),...  62.5 us
    all_gather x1, waiting for transfers between devices, body(): gathered = lax.all_gather(snapshots, 'snap', axis=1, tiled=True)  46.7 us
    gather x1, local copies, waits for them, and re-layouts, body(): ordered = jnp.take(eigvec, time_index, axis=0)  7.5 us
  transfers between devices with their start and end apart: 3, of which 3 were waited for; matrix products, arithmetic and copies ran while one was open for 4% of the time, Pallas kernels for 0%

commit v1 on v0

v1 whole, which is shorter than its diff:
```python
import jax
import jax.numpy as jnp
from jax import lax
from jax.experimental import pallas as pl
from jax.experimental.pallas import tpu as pltpu
from jax.sharding import Mesh, PartitionSpec as P

SWAP = [(0, 1), (1, 0)]


def gram_kernel(same_ref, other_ref, weighted_ref, out_ref):
    core = lax.axis_index("core")
    weighted = weighted_ref[...]
    for rows_ref, core1 in ((same_ref, core), (other_ref, 1 - core)):
        for x1 in range(4):
            part = lax.dot_general(
                rows_ref[x1], weighted, (((0,), (0,)), ((), ())), preferred_element_type=jnp.float32
            ).astype(jnp.bfloat16)
            for y2 in range(2):
                for half in range(2):
                    out_ref[y2 * 4 + core1 * 2 + half, x1] = part[
                        half * 64 : half * 64 + 64, y2 * 128 : y2 * 128 + 128
                    ]


def modes_kernel(same_ref, other_ref, ordered_ref, out_ref):
    core = lax.axis_index("core")
    total = jnp.zeros(out_ref.shape, jnp.float32)
    for rows_ref, core1 in ((same_ref, core), (other_ref, 1 - core)):
        for x1 in range(4):
            total += lax.dot_general(
                ordered_ref[core1, x1], rows_ref[x1], (((1,), (1,)), ((), ())), preferred_element_type=jnp.float32
            )
    out_ref[...] = total


def body(snapshots, cell_weight, eigvec, time_index):
    rows, width = snapshots.shape
    y, x, core = lax.axis_index("yl"), lax.axis_index("x"), lax.axis_index("core")
    scaling = 1.0 / (rows * lax.axis_size("z") * lax.axis_size("yh"))

    partner = lax.ppermute(snapshots, "yl", SWAP)
    same = lax.all_to_all(jnp.broadcast_to(snapshots[None], (4, rows, width)), "x", 0, 0, tiled=True)
    same, partner = lax.optimization_barrier((same, partner))
    other = lax.ppermute(same, "core", SWAP)

    index = lax.dynamic_slice_in_dim(time_index, y * 1024, 1024, 0)
    ordered = jnp.take(eigvec, index, axis=0)
    ordered = ordered.reshape(4, 2, 128, 2, 8, 16)
    ordered = lax.dynamic_index_in_dim(ordered, x * 2 + core, 4, keepdims=False)
    ordered = ordered.transpose(1, 0, 3, 4, 2).reshape(2, 4, 32, 128)

    first = jnp.where(y == 0, snapshots, partner).astype(jnp.float32)
    second = jnp.where(y == 0, partner, snapshots).astype(jnp.float32)
    weighted = (jnp.concatenate([first, second], 1) * cell_weight[:, None]).astype(jnp.bfloat16)

    vmem = pl.BlockSpec(memory_space=pltpu.VMEM)
    parts = pl.pallas_call(
        gram_kernel,
        out_shape=jax.ShapeDtypeStruct((8, 4, 64, 128), jnp.bfloat16),
        in_specs=[vmem] * 3,
        out_specs=vmem,
        compiler_params=pltpu.CompilerParams(vmem_limit_bytes=32 * 1024 * 1024),
        name="gram_parts",
    )(same, other, weighted)
    mode_part = pl.pallas_call(
        modes_kernel,
        out_shape=jax.ShapeDtypeStruct((32, rows), jnp.float32),
        in_specs=[vmem] * 3,
        out_specs=vmem,
        compiler_params=pltpu.CompilerParams(vmem_limit_bytes=32 * 1024 * 1024),
        name="mode_parts",
    )(same, other, ordered)

    parts = lax.all_to_all(parts, ("yl", "yh"), 0, 0, tiled=True)
    mode_part = mode_part.reshape(2, 16, rows)
    away = lax.ppermute(lax.dynamic_index_in_dim(mode_part, 1 - y, 0, keepdims=False), "yl", SWAP)
    modes = lax.dynamic_index_in_dim(mode_part, y, 0, keepdims=False) + away

    parts = jnp.sum(parts.reshape(2, 4, 4, 64, 128).astype(jnp.float32), axis=1)
    parts = lax.all_to_all(parts.reshape(8, 64, 128), "z", 0, 0, tiled=True)
    gram = jnp.sum(parts, axis=0) * scaling
    return gram, modes


def solution(mesh):
    fine = Mesh(mesh.devices.reshape(2, 4, 2, 8, 4), ("yl", "x", "core", "z", "yh"))
    snap, space = ("yl", "x", "core"), ("z", "yh")
    in_specs = (P(space, snap), P(space), P(), P())
    out_specs = (P(space, snap), P(snap, space))
    return jax.shard_map(body, mesh=fine, in_specs=in_specs, out_specs=out_specs, check_vma=False)
```

time: 371 us -> 78.4 us (0.21)
  the two profiles are of different devices: /device:TPU:6 before, /device:TPU:8 now
where the time goes in v1:
time: 78.4 us; the launch traced here: 77.7 us
  starting transfers between devices  33.2 us (42%)
  waiting for transfers between devices  23 us (29%)
  local copies, waits for them, and re-layouts  13 us (17%)
  other arithmetic  6.18 us (8%)
  Pallas kernels  1.52 us (2%)
    all_to_all x1, starting transfers between devices, body(): parts = lax.all_to_all(parts.reshape(8, 64, 128), 'z', 0, 0, tiled=True)  10.3 us
    gather x3, local copies, waits for them, and re-layouts, body(): ordered = jnp.take(eigvec, index, axis=0)  9.27 us
    all_to_all x1, starting transfers between devices, body(): parts = lax.all_to_all(parts, ('yl', 'yh'), 0, 0, tiled=True)  7.68 us
    all_to_all x1, waiting for transfers between devices, body(): parts = lax.all_to_all(parts, ('yl', 'yh'), 0, 0, tiled=True)  7.12 us
    ppermute x1, starting transfers between devices, body(): partner = lax.ppermute(snapshots, 'yl', SWAP)  6.97 us
    all_to_all x1, starting transfers between devices, body(): lax.all_to_all(jnp.broadcast_to(snapshots[None], (4, rows, width)), 'x',...  4.42 us
    ppermute x1, waiting for transfers between devices, body(): partner = lax.ppermute(snapshots, 'yl', SWAP)  4.34 us
    ppermute x1, waiting for transfers between devices, body(): lax.ppermute(lax.dynamic_index_in_dim(mode_part, 1 - y, 0, keepdims=False...  4.23 us
  transfers between devices with their start and end apart: 6, of which 6 were waited for; matrix products, arithmetic and copies ran while one was open for 16% of the time, Pallas kernels for 1%

profile of v1, /device:TPU:8, one launch (start us, length us, event | category | flops | bytes accessed | tf_op | source)
XLA Modules:
  0.0 77.7 jit_solution(4262560329470592646)
XLA Ops:
  0.6 0.0 copy-start
  0.6 2.1 %broadcast_in_dim.21 = bf16[4,1024,128]{2,1,0:T(8,128)(2,1)} broadcast(bf16[1024,128]{1,0:T(8,128)(2,1)} %param.4), dimensions={1,2} | broadcast | bytes 1310720 | tf_op jit(solution)/shard_map/broadcast_in_dim | solution.py:43
  2.8 0.0 copy-start.2
  2.8 4.4 %all-to-all-start = ((bf16[4,1024,128]{2,1,0:T(8,128)(2,1)}), bf16[4,1024,128]{2,1,0:T(8,128)(2,1)S(1)}, u32[]{:S(2)}, u32[]{:S(2)}) async-start(bf16[4,1024,128]{2,1,0:T(8,128)(2,1)} %broadcast_in_dim.21), calls=%async_computation | async-start | bytes 2097152 | tf_op jit(solution)/shard_map/all_to_all | solution.py:43
  7.2 0.0 copy-done.2
  7.2 7.0 %collective-permute-start = (bf16[1024,128]{1,0:T(8,128)(2,1)S(1)}, bf16[1024,128]{1,0:T(8,128)(2,1)S(1)}, u32[]{:S(2)}, u32[]{:S(2)}) collective-permute-start(bf16[1024,128]{1,0:T(8,128)(2,1)S(1)} %copy-done.2), channel_id=1, source_target_pairs={{0,256},{256,0},{1,257},{257,1},{2,258},{258,2},{3,259},{259,3},{4... | collective-permute-start | bytes 786440 | tf_op jit(solution)/shard_map/ppermute | solution.py:42
  14.2 4.3 %collective-permute-done = bf16[1024,128]{1,0:T(8,128)(2,1)S(1)} collective-permute-done((bf16[1024,128]{1,0:T(8,128)(2,1)S(1)}, bf16[1024,128]{1,0:T(8,128)(2,1)S(1)}, u32[]{:S(2)}, u32[]{:S(2)}) %collective-permute-start) | collective-permute-done | bytes 262176 | tf_op jit(solution)/shard_map/ppermute | solution.py:42
  18.5 0.0 copy-start.3
  18.5 0.7 copy-done.3
  19.2 3.1 %all-to-all-done.same_ref = bf16[4,1024,128]{2,1,0:T(8,128)(2,1)S(1)} async-done(((bf16[4,1024,128]{2,1,0:T(8,128)(2,1)}), bf16[4,1024,128]{2,1,0:T(8,128)(2,1)S(1)}, u32[]{:S(2)}, u32[]{:S(2)}) %all-to-all-start) | async-done | bytes 1048608 | tf_op jit(solution)/shard_map/all_to_all | solution.py:43
  22.3 1.9 %collective-permute-start.1 = (bf16[4,1024,128]{2,1,0:T(8,128)(2,1)S(1)}, bf16[4,1024,128]{2,1,0:T(8,128)(2,1)S(1)}, u32[]{:S(2)}, u32[]{:S(2)}) collective-permute-start(bf16[4,1024,128]{2,1,0:T(8,128)(2,1)S(1)} %all-to-all-done.same_ref), channel_id=1, source_target_pairs={{0,32},{32,0},{1,33},{33,1},{2,34},{34,2},{3,35},{35,3},{4,36},{36... | collective-permute-start | bytes 3145736 | tf_op jit(solution)/shard_map/ppermute | solution.py:45
  24.2 0.0 copy-start.5
  24.3 1.0 %broadcast_select_fusion.1 = (bf16[1024,128]{1,0:T(8,128)(2,1)S(1)}, bf16[1024,128]{1,0:T(8,128)(2,1)S(1)}) fusion(bf16[1024,128]{1,0:T(8,128)(2,1)S(1)} %copy-done.2, bf16[1024,128]{1,0:T(8,128)(2,1)} %copy-done.3, pred[]{:T(512)S(6)} %eq.4), kind=kLoop, calls=%fused_computation.4 | loop fusion | flops 262144 | bytes 1048577 | tf_op jit(solution)/shard_map/jit(_where)/select_n | solution.py:53
  25.2 0.0 copy-done.5
  25.3 0.2 multiply_convert_fusion.weighted_ref
  25.5 1.4 %collective-permute-done.1.other_ref = bf16[4,1024,128]{2,1,0:T(8,128)(2,1)S(1)} collective-permute-done((bf16[4,1024,128]{2,1,0:T(8,128)(2,1)S(1)}, bf16[4,1024,128]{2,1,0:T(8,128)(2,1)S(1)}, u32[]{:S(2)}, u32[]{:S(2)}) %collective-permute-start.1) | collective-permute-done | bytes 1048608 | tf_op jit(solution)/shard_map/ppermute | solution.py:45
  26.9 0.8 gram_parts.1
  27.6 0.0 copy-start.1
  27.6 0.8 copy-done.1
  28.4 0.0 copy-start.4
  28.4 7.7 %all-to-all-start.1 = ((bf16[8,4,64,128]{3,2,1,0:T(8,128)(2,1)}), bf16[8,4,64,128]{3,2,1,0:T(8,128)(2,1)}, u32[]{:S(2)}, u32[]{:S(2)}) async-start(bf16[8,4,64,128]{3,2,1,0:T(8,128)(2,1)} %copy-done.1), calls=%async_computation.1 | async-start | bytes 1048576 | tf_op jit(solution)/shard_map/all_to_all | solution.py:75
  36.1 0.0 copy-done.4
  36.1 0.0 copy-done
  36.1 5.0 %gather_fusion = bf16[1024,256]{1,0:T(8,128)(2,1)} fusion(bf16[2048,256]{1,0:T(8,128)(2,1)S(1)} %copy-done, s32[1024]{0:T(1024)S(1)} %fusion), kind=kCustom, calls=%fused_computation | custom fusion | bytes 1052672 | tf_op jit(solution)/shard_map/jit(_take)/gather | solution.py:48
  41.1 2.0 %copy.11 = bf16[1024,256]{0,1:T(8,128)(2,1)} copy(bf16[1024,256]{1,0:T(8,128)(2,1)} %gather_fusion) | data formatting | bytes 1048576 | tf_op jit(solution)/shard_map/jit(_take)/gather | solution.py:48
  43.2 2.2 %gather.7 = bf16[4,2,128,2,8,16]{2,1,0,5,4,3:T(2,128)(2,1)} reshape(bf16[1024,256]{0,1:T(8,128)(2,1)} %copy.11) | data formatting | bytes 1048576 | tf_op jit(solution)/shard_map/jit(_take)/gather | solution.py:48
  45.4 7.1 %all-to-all-done.1 = bf16[8,4,64,128]{3,2,1,0:T(8,128)(2,1)} async-done(((bf16[8,4,64,128]{3,2,1,0:T(8,128)(2,1)}), bf16[8,4,64,128]{3,2,1,0:T(8,128)(2,1)}, u32[]{:S(2)}, u32[]{:S(2)}) %all-to-all-start.1) | async-done | bytes 524320 | tf_op jit(solution)/shard_map/all_to_all | solution.py:75
  52.5 1.8 %convert_reduce_fusion = f32[2,4,64,128]{3,2,1,0:T(8,128)} fusion(bf16[8,4,64,128]{3,2,1,0:T(8,128)(2,1)} %all-to-all-done.1), kind=kLoop, calls=%fused_computation.1 | loop fusion | flops 458752 | bytes 786432 | tf_op jit(solution)/shard_map/reduce_sum | solution.py:80
  54.4 10.3 %all-to-all-start.2 = ((f32[8,64,128]{2,1,0:T(8,128)}), f32[8,64,128]{2,1,0:T(8,128)}, u32[]{:S(2)}, u32[]{:S(2)}) async-start(f32[8,64,128]{2,1,0:T(8,128)} %bitcast.1), calls=%async_computation.2 | async-start | bytes 524288 | tf_op jit(solution)/shard_map/all_to_all | solution.py:81
  64.7 0.9 %broadcast_select_fusion.2 = bf16[4,2,128,2,1,16]{2,1,0,5,4,3:T(2,128)(2,1)S(1)} fusion(pred[4,2,128]{2,1,0:T(4,128)(4,1)S(1)} %broadcast_in_dim.22, bf16[4,2,128,2,8,16]{2,1,0,5,4,3:T(2,128)(2,1)} %gather.7, s32[]{:T(128)S(6)} %select_n.42), kind=kLoop, calls=%fused_computation.5 | loop fusion | flops 32768 | bytes 132100 | tf_op jit(solution)/shard_map/jit(_take)/select_n | solution.py:48
  65.6 0.8 mode_parts.1
  66.4 1.9 %collective-permute-start.2 = (f32[16,1024]{1,0:T(8,128)S(1)}, f32[16,1024]{1,0:T(8,128)S(1)}, u32[]{:S(2)}, u32[]{:S(2)}) collective-permute-start(f32[16,1024]{1,0:T(8,128)S(1)} %dynamic-slice_bitcast_fusion), channel_id=1, source_target_pairs={{0,256},{256,0},{1,257},{257,1},{2,258},{258,2},{3,259},{259,3},{4... | collective-permute-start | bytes 196616 | tf_op jit(solution)/shard_map/ppermute | solution.py:77
  68.3 4.2 %collective-permute-done.2 = f32[16,1024]{1,0:T(8,128)S(1)} collective-permute-done((f32[16,1024]{1,0:T(8,128)S(1)}, f32[16,1024]{1,0:T(8,128)S(1)}, u32[]{:S(2)}, u32[]{:S(2)}) %collective-permute-start.2) | collective-permute-done | bytes 65568 | tf_op jit(solution)/shard_map/ppermute | solution.py:77
  72.6 0.6 bitcast_add_fusion
  73.2 2.9 %all-to-all-done.2 = f32[8,64,128]{2,1,0:T(8,128)} async-done(((f32[8,64,128]{2,1,0:T(8,128)}), f32[8,64,128]{2,1,0:T(8,128)}, u32[]{:S(2)}, u32[]{:S(2)}) %all-to-all-start.2) | async-done | bytes 262176 | tf_op jit(solution)/shard_map/all_to_all | solution.py:81
  76.1 1.0 %reduce_sum.19 = f32[64,128]{1,0:T(8,128)S(1)} reduce(f32[8,64,128]{2,1,0:T(8,128)} %all-to-all-done.2, f32[]{:T(128)} %constant.44.clone.1), dimensions={0}, to_apply=%region_1.2 | reduce | flops 57344 | bytes 294916 | tf_op jit(solution)/shard_map/reduce_sum | solution.py:82
  77.1 0.6 broadcast_multiply_fusion
  (5 shorter events, 0.1 us)
Async XLA Ops:
  0.6 35.5 %copy-start = (bf16[2048,256]{1,0:T(8,128)(2,1)S(1)}, bf16[2048,256]{1,0:T(8,128)(2,1)}, u32[]{:S(2)}) copy-start(bf16[2048,256]{1,0:T(8,128)(2,1)} %param.6) | copy-start | bytes 3145732
  2.8 4.4 %copy-start.2 = (bf16[1024,128]{1,0:T(8,128)(2,1)S(1)}, bf16[1024,128]{1,0:T(8,128)(2,1)}, u32[]{:S(2)}) copy-start(bf16[1024,128]{1,0:T(8,128)(2,1)} %param.4) | copy-start | bytes 786436
  2.8 19.5 %all-to-all-start = ((bf16[4,1024,128]{2,1,0:T(8,128)(2,1)}), bf16[4,1024,128]{2,1,0:T(8,128)(2,1)S(1)}, u32[]{:S(2)}, u32[]{:S(2)}) async-start(bf16[4,1024,128]{2,1,0:T(8,128)(2,1)} %broadcast_in_dim.21), calls=%async_computation | async-start | bytes 2097152 | tf_op jit(solution)/shard_map/all_to_all | solution.py:43
  7.2 11.3 %collective-permute-start = (bf16[1024,128]{1,0:T(8,128)(2,1)S(1)}, bf16[1024,128]{1,0:T(8,128)(2,1)S(1)}, u32[]{:S(2)}, u32[]{:S(2)}) collective-permute-start(bf16[1024,128]{1,0:T(8,128)(2,1)S(1)} %copy-done.2), channel_id=1, source_target_pairs={{0,256},{256,0},{1,257},{257,1},{2,258},{258,2},{3,259},{259,3},{4... | collective-permute-start | bytes 786440 | tf_op jit(solution)/shard_map/ppermute | solution.py:42
  18.5 0.7 copy-start.3
  22.3 4.5 %collective-permute-start.1 = (bf16[4,1024,128]{2,1,0:T(8,128)(2,1)S(1)}, bf16[4,1024,128]{2,1,0:T(8,128)(2,1)S(1)}, u32[]{:S(2)}, u32[]{:S(2)}) collective-permute-start(bf16[4,1024,128]{2,1,0:T(8,128)(2,1)S(1)} %all-to-all-done.same_ref), channel_id=1, source_target_pairs={{0,32},{32,0},{1,33},{33,1},{2,34},{34,2},{3,35},{35,3},{4,36},{36... | collective-permute-start | bytes 3145736 | tf_op jit(solution)/shard_map/ppermute | solution.py:45
  24.2 1.0 %copy-start.5 = (f32[1024]{0:T(1024)S(1)}, f32[1024]{0:T(1024)}, u32[]{:S(2)}) copy-start(f32[1024]{0:T(1024)} %param.5) | copy-start | bytes 12292
  27.6 0.8 %copy-start.1 = (bf16[8,4,64,128]{3,2,1,0:T(8,128)(2,1)}, bf16[8,4,64,128]{3,2,1,0:T(8,128)(2,1)S(1)}, u32[]{:S(2)}) copy-start(bf16[8,4,64,128]{3,2,1,0:T(8,128)(2,1)S(1)} %gram_parts.1) | copy-start | bytes 1572868
  28.4 7.7 %copy-start.4 = (s32[2048]{0:T(1024)S(1)}, s32[2048]{0:T(1024)}, u32[]{:S(2)}) copy-start(s32[2048]{0:T(1024)} %param.7) | copy-start | bytes 24580
  28.4 24.1 %all-to-all-start.1 = ((bf16[8,4,64,128]{3,2,1,0:T(8,128)(2,1)}), bf16[8,4,64,128]{3,2,1,0:T(8,128)(2,1)}, u32[]{:S(2)}, u32[]{:S(2)}) async-start(bf16[8,4,64,128]{3,2,1,0:T(8,128)(2,1)} %copy-done.1), calls=%async_computation.1 | async-start | bytes 1048576 | tf_op jit(solution)/shard_map/all_to_all | solution.py:75
  54.4 21.7 %all-to-all-start.2 = ((f32[8,64,128]{2,1,0:T(8,128)}), f32[8,64,128]{2,1,0:T(8,128)}, u32[]{:S(2)}, u32[]{:S(2)}) async-start(f32[8,64,128]{2,1,0:T(8,128)} %bitcast.1), calls=%async_computation.2 | async-start | bytes 524288 | tf_op jit(solution)/shard_map/all_to_all | solution.py:81
  66.4 6.2 %collective-permute-start.2 = (f32[16,1024]{1,0:T(8,128)S(1)}, f32[16,1024]{1,0:T(8,128)S(1)}, u32[]{:S(2)}, u32[]{:S(2)}) collective-permute-start(f32[16,1024]{1,0:T(8,128)S(1)} %dynamic-slice_bitcast_fusion), channel_id=1, source_target_pairs={{0,256},{256,0},{1,257},{257,1},{2,258},{258,2},{3,259},{259,3},{4... | collective-permute-start | bytes 196616 | tf_op jit(solution)/shard_map/ppermute | solution.py:77

commit v2 on v0

v2 whole, which is shorter than its diff:
```python
import jax
import jax.numpy as jnp
from jax import lax
from jax.experimental import pallas as pl
from jax.experimental.pallas import tpu as pltpu
from jax.sharding import Mesh, PartitionSpec as P

SWAP = [(0, 1), (1, 0)]
VMEM = pl.BlockSpec(memory_space=pltpu.VMEM)


def local(kernel, out_shape, *operands, name):
    outs = jax.tree.map(lambda _: VMEM, out_shape)
    return pl.pallas_call(
        kernel,
        out_shape=out_shape,
        in_specs=[VMEM] * len(operands),
        out_specs=outs,
        compiler_params=pltpu.CompilerParams(vmem_limit_bytes=32 * 1024 * 1024),
        name=name,
    )(*operands)


def ordered_kernel(index_ref, eigvec_ref, out_ref):
    y, x, core = lax.axis_index("yl"), lax.axis_index("x"), lax.axis_index("core")
    times, modes = eigvec_ref.shape
    row = lax.broadcasted_iota(jnp.int32, (32, modes), 0)
    column = lax.broadcasted_iota(jnp.int32, (32, modes), 1)
    wanted = (row // 16) * 128 + (x * 2 + core) * 16 + row % 16
    chosen = (column == wanted).astype(jnp.float32).astype(jnp.bfloat16)
    kept = lax.dot_general(
        chosen, eigvec_ref[...], (((1,), (1,)), ((), ())), preferred_element_type=jnp.float32
    ).astype(jnp.bfloat16)
    time = lax.broadcasted_iota(jnp.int32, (times, 128), 0)
    for x1 in range(4):
        for core1 in range(2):
            index = index_ref[pl.ds(y * 8 + x1 * 2 + core1, 1), :]
            hot = (time == index).astype(jnp.float32).astype(jnp.bfloat16)
            out_ref[core1, x1] = jnp.dot(kept, hot, preferred_element_type=jnp.float32).astype(jnp.bfloat16)


def shifts():
    x = lax.axis_index("x")
    return x, (x + 3) % 4, (x + 1) % 4, (x + 2) % 4


def stack_kernel(*refs):
    for k, block in enumerate(refs[:-1]):
        refs[-1][k] = block[...]


def gram_blocks(rows_ref, weighted_ref, store):
    weighted = weighted_ref[...]
    for k in range(4):
        part = lax.dot_general(
            rows_ref[k], weighted, (((0,), (0,)), ((), ())), preferred_element_type=jnp.float32
        ).astype(jnp.bfloat16)
        for side in range(2):
            for half in range(2):
                store(side, half, k, part[half * 64 : half * 64 + 64, side * 128 : side * 128 + 128])


def gram_same_kernel(rows_ref, weighted_ref, out_ref):
    def store(side, half, k, tile):
        out_ref[side * 2 + half, k] = tile

    gram_blocks(rows_ref, weighted_ref, store)


def gram_other_kernel(rows_ref, weighted_ref, begun_ref, out_ref):
    y, core = lax.axis_index("yl"), lax.axis_index("core")
    places = shifts()

    def place(side, half, core1):
        return (y if side == 0 else 1 - y) * 4 + core1 * 2 + half

    for k in range(4):
        for side in range(2):
            for half in range(2):
                out_ref[place(side, half, core), places[k]] = begun_ref[side * 2 + half, k]

    def store(side, half, k, tile):
        out_ref[place(side, half, 1 - core), places[k]] = tile

    gram_blocks(rows_ref, weighted_ref, store)


def modes_blocks(rows_ref, ordered_ref, core1):
    total = None
    for k, x1 in enumerate(shifts()):
        part = lax.dot_general(
            ordered_ref[core1, x1], rows_ref[k], (((1,), (1,)), ((), ())), preferred_element_type=jnp.float32
        )
        total = part if total is None else total + part
    return total


def modes_same_kernel(rows_ref, ordered_ref, out_ref):
    out_ref[...] = modes_blocks(rows_ref, ordered_ref, lax.axis_index("core"))


def modes_other_kernel(rows_ref, ordered_ref, begun_ref, away_ref, stay_ref):
    total = begun_ref[...] + modes_blocks(rows_ref, ordered_ref, 1 - lax.axis_index("core"))
    first = lax.axis_index("yl") == 0
    stay_ref[...] = jnp.where(first, total[:16], total[16:])
    away_ref[...] = jnp.where(first, total[16:], total[:16])


def sum_kernel(scaling, parts_ref, out_ref):
    for y1 in range(2):
        for x1 in range(4):
            total = parts_ref[y1 * 4, x1].astype(jnp.float32)
            for k in range(1, 4):
                total += parts_ref[y1 * 4 + k, x1].astype(jnp.float32)
            out_ref[y1 * 4 + x1] = total * scaling


def last_kernel(parts_ref, stay_ref, away_ref, gram_ref, modes_ref):
    total = parts_ref[0]
    for k in range(1, 8):
        total += parts_ref[k]
    gram_ref[...] = total
    modes_ref[...] = stay_ref[...] + away_ref[...]


def body(snapshots, cell_weight, eigvec, time_index):
    rows, width = snapshots.shape
    scaling = 1.0 / (rows * lax.axis_size("z") * lax.axis_size("yh"))
    shape = jax.ShapeDtypeStruct

    def shift(k):
        return lax.ppermute(snapshots, "x", [(i, (i + k) % 4) for i in range(4)])

    across, ahead, behind = shift(2), shift(1), shift(3)
    partner = lax.ppermute(snapshots, "yl", SWAP)
    weighted = (jnp.concatenate([snapshots, partner], 1).astype(jnp.float32) * cell_weight[:, None]).astype(
        jnp.bfloat16
    )
    ordered = local(
        ordered_kernel, shape((2, 4, 32, 128), jnp.bfloat16), time_index.reshape(16, 128), eigvec, name="ordered"
    )
    across, ahead, behind, weighted, ordered = lax.optimization_barrier((across, ahead, behind, weighted, ordered))
    stacked = shape((4, rows, width), jnp.bfloat16)
    same = local(stack_kernel, stacked, snapshots, ahead, behind, across, name="stack")
    other = lax.ppermute(same, "core", SWAP)
    begun = local(gram_same_kernel, shape((4, 4, 64, 128), jnp.bfloat16), same, weighted, name="gram_same")
    modes = local(modes_same_kernel, shape((32, rows), jnp.float32), same, ordered, name="modes_same")
    other, begun, modes = lax.optimization_barrier((other, begun, modes))
    parts = local(
        gram_other_kernel, shape((8, 4, 64, 128), jnp.bfloat16), other, weighted, begun, name="gram_other"
    )
    parts = lax.all_to_all(parts, ("yl", "yh"), 0, 0, tiled=True)
    parts = local(lambda *refs: sum_kernel(scaling, *refs), shape((8, 64, 128), jnp.float32), parts, name="sum_y")
    parts, other, ordered, modes = lax.optimization_barrier((parts, other, ordered, modes))
    parts = lax.all_to_all(parts, "z", 0, 0, tiled=True)
    half = shape((16, rows), jnp.float32)
    away, stay = local(modes_other_kernel, [half, half], other, ordered, modes, name="modes_other")
    away = lax.ppermute(away, "yl", SWAP)
    outs = [shape((64, 128), jnp.float32), half]
    gram, modes = local(last_kernel, outs, parts, stay, away, name="sum_z")
    return gram, modes


def solution(mesh):
    fine = Mesh(mesh.devices.reshape(2, 4, 2, 8, 4), ("yl", "x", "core", "z", "yh"))
    snap, space = ("yl", "x", "core"), ("z", "yh")
    in_specs = (P(space, snap), P(space), P(), P())
    out_specs = (P(space, snap), P(snap, space))
    return jax.shard_map(body, mesh=fine, in_specs=in_specs, out_specs=out_specs, check_vma=False)
```

time: 371 us -> 72.6 us (0.20)
  the two profiles are of different devices: /device:TPU:6 before, /device:TPU:14 now
where the time goes in v2:
time: 72.6 us; the launch traced here: 72.1 us
  starting transfers between devices  29 us (40%)
  blocking collectives  22.4 us (31%)
  waiting for transfers between devices  13 us (18%)
  Pallas kernels  4.85 us (7%)
  local copies, waits for them, and re-layouts  1.92 us (3%)
  between operations  0.77 us (1%)
    all_to_all x1, blocking collectives, body(): parts = lax.all_to_all(parts, ('yl', 'yh'), 0, 0, tiled=True)  22.4 us
    ppermute x3, starting transfers between devices, shift(): return lax.ppermute(snapshots, 'x', [(i, (i + k) % 4) for i in range(4)])  12.4 us
    all_to_all x1, starting transfers between devices, body(): parts = lax.all_to_all(parts, 'z', 0, 0, tiled=True)  10.3 us
    pallas_call x8, Pallas kernels, local(): pl.pallas_call(kernel, out_shape=out_shape, in_specs=[VMEM] * len(operand...  4.85 us
    ppermute x1, waiting for transfers between devices, body(): away = lax.ppermute(away, 'yl', SWAP)  4.23 us
    all_to_all x1, waiting for transfers between devices, body(): parts = lax.all_to_all(parts, 'z', 0, 0, tiled=True)  3.88 us
    ppermute x3, waiting for transfers between devices, shift(): return lax.ppermute(snapshots, 'x', [(i, (i + k) % 4) for i in range(4)])  3.2 us
    ppermute x1, starting transfers between devices, body(): partner = lax.ppermute(snapshots, 'yl', SWAP)  2.36 us
  transfers between devices with their start and end apart: 7, of which 4 were waited for; matrix products, arithmetic and copies ran while one was open for 0% of the time, Pallas kernels for 4%

profile of v2, /device:TPU:14, one launch (start us, length us, event | category | flops | bytes accessed | tf_op | source)
XLA Modules:
  0.0 72.1 jit_solution(5519493714069372109)
XLA Ops:
  0.6 2.4 %collective-permute-start.3 = (bf16[1024,128]{1,0:T(8,128)(2,1)}, bf16[1024,128]{1,0:T(8,128)(2,1)S(1)}, u32[]{:S(2)}, u32[]{:S(2)}) collective-permute-start(bf16[1024,128]{1,0:T(8,128)(2,1)} %refs_0_.1), channel_id=1, source_target_pairs={{0,256},{256,0},{1,257},{257,1},{2,258},{258,2},{3,259},{259,3},{4... | collective-permute-start | bytes 786440 | tf_op jit(solution)/shard_map/ppermute | solution.py:135
  3.0 3.3 %collective-permute-start = (bf16[1024,128]{1,0:T(8,128)(2,1)}, bf16[1024,128]{1,0:T(8,128)(2,1)S(1)}, u32[]{:S(2)}, u32[]{:S(2)}) collective-permute-start(bf16[1024,128]{1,0:T(8,128)(2,1)} %refs_0_.1), channel_id=1, source_target_pairs={{0,128},{64,192},{128,0},{192,64},{1,129},{65,193},{129,1},{193,65... | collective-permute-start | bytes 786440 | tf_op jit(solution)/shard_map/ppermute | solution.py:132
  6.3 6.4 %collective-permute-start.1 = (bf16[1024,128]{1,0:T(8,128)(2,1)}, bf16[1024,128]{1,0:T(8,128)(2,1)S(1)}, u32[]{:S(2)}, u32[]{:S(2)}) collective-permute-start(bf16[1024,128]{1,0:T(8,128)(2,1)} %refs_0_.1), channel_id=1, source_target_pairs={{0,64},{64,128},{128,192},{192,0},{1,65},{65,129},{129,193},{193,1... | collective-permute-start | bytes 786440 | tf_op jit(solution)/shard_map/ppermute | solution.py:132
  12.7 2.8 %collective-permute-start.2 = (bf16[1024,128]{1,0:T(8,128)(2,1)}, bf16[1024,128]{1,0:T(8,128)(2,1)S(1)}, u32[]{:S(2)}, u32[]{:S(2)}) collective-permute-start(bf16[1024,128]{1,0:T(8,128)(2,1)} %refs_0_.1), channel_id=1, source_target_pairs={{0,192},{64,0},{128,64},{192,128},{1,193},{65,1},{129,65},{193,129... | collective-permute-start | bytes 786440 | tf_op jit(solution)/shard_map/ppermute | solution.py:132
  15.5 0.0 copy-start
  15.5 1.2 %copy-done = bf16[2048,256]{1,0:T(8,128)(2,1)S(1)} copy-done((bf16[2048,256]{1,0:T(8,128)(2,1)S(1)}, bf16[2048,256]{1,0:T(8,128)(2,1)}, u32[]{:S(2)}) %copy-start) | copy-done | bytes 1048600
  16.7 0.0 copy-start.2
  16.7 0.7 copy-done.2
  17.4 0.0 copy-start.1
  17.4 0.0 copy-start.3
  17.4 1.5 %ordered.1.ordered_ref = bf16[2,4,32,128]{3,2,1,0:T(8,128)(2,1)S(1)} custom-call(s32[16,128]{1,0:T(8,128)S(1)} %bitcast.1, bf16[2048,256]{1,0:T(8,128)(2,1)S(1)} %copy-done), custom_call_target="tpu_custom_call" | custom-call | tf_op jit(solution)/shard_map/ordered/pallas_call | solution.py:14
  18.9 0.0 collective-permute-done.3
  18.9 0.0 copy-done.1
  18.9 0.0 copy-done.3
  19.0 0.2 multiply_convert_fusion.weighted_ref
  19.2 0.0 collective-permute-done.refs_3_
  19.2 0.0 collective-permute-done.1.refs_1_
  19.2 3.2 %collective-permute-done.2.refs_2_ = bf16[1024,128]{1,0:T(8,128)(2,1)S(1)} collective-permute-done((bf16[1024,128]{1,0:T(8,128)(2,1)}, bf16[1024,128]{1,0:T(8,128)(2,1)S(1)}, u32[]{:S(2)}, u32[]{:S(2)}) %collective-permute-start.2) | collective-permute-done | bytes 262176 | tf_op jit(solution)/shard_map/ppermute | solution.py:132
  22.4 0.1 stack.1.rows_ref
  22.4 1.9 %collective-permute-start.4 = (bf16[4,1024,128]{2,1,0:T(8,128)(2,1)S(1)}, bf16[4,1024,128]{2,1,0:T(8,128)(2,1)S(1)}, u32[]{:S(2)}, u32[]{:S(2)}) collective-permute-start(bf16[4,1024,128]{2,1,0:T(8,128)(2,1)S(1)} %stack.1.rows_ref), channel_id=1, source_target_pairs={{0,32},{32,0},{1,33},{33,1},{2,34},{34,2},{3,35},{35,3},{4,36},{36... | collective-permute-start | bytes 3145736 | tf_op jit(solution)/shard_map/ppermute | solution.py:145
  24.4 0.5 gram_same.1.begun_ref
  24.9 0.4 modes_same.1.begun_ref
  25.3 1.7 %collective-permute-done.4.rows_ref = bf16[4,1024,128]{2,1,0:T(8,128)(2,1)S(1)} collective-permute-done((bf16[4,1024,128]{2,1,0:T(8,128)(2,1)S(1)}, bf16[4,1024,128]{2,1,0:T(8,128)(2,1)S(1)}, u32[]{:S(2)}, u32[]{:S(2)}) %collective-permute-start.4) | collective-permute-done | bytes 1048608 | tf_op jit(solution)/shard_map/ppermute | solution.py:145
  27.0 0.5 gram_other.1
  27.5 22.4 %all_to_all.10.refs_0_ = bf16[8,4,64,128]{3,2,1,0:T(8,128)(2,1)S(1)} all-to-all(bf16[8,4,64,128]{3,2,1,0:T(8,128)(2,1)S(1)} %gram_other.1), channel_id=1, replica_groups=mesh['yl'=2,'x'=4,'core'=2,'z'=8,'yh'=4] {'yl','yh'}, dimensions={0} | all-to-all | bytes 1048576 | tf_op jit(solution)/shard_map/all_to_all | solution.py:152
  49.9 0.8 %sum_y.1 = f32[8,64,128]{2,1,0:T(8,128)} custom-call(bf16[8,4,64,128]{3,2,1,0:T(8,128)(2,1)S(1)} %all_to_all.10.refs_0_), custom_call_target="tpu_custom_call" | custom-call | tf_op jit(solution)/shard_map/sum_y/pallas_call | solution.py:14
  50.6 10.3 %all-to-all-start.1 = ((f32[8,64,128]{2,1,0:T(8,128)}), f32[8,64,128]{2,1,0:T(8,128)S(1)}, u32[]{:S(2)}, u32[]{:S(2)}) async-start(f32[8,64,128]{2,1,0:T(8,128)} %sum_y.1), calls=%async_computation.1 | async-start | bytes 524288 | tf_op jit(solution)/shard_map/all_to_all | solution.py:155
  61.0 0.4 modes_other.1
  61.4 1.9 %collective-permute-start.5 = (f32[16,1024]{1,0:T(8,128)S(1)}, f32[16,1024]{1,0:T(8,128)S(1)}, u32[]{:S(2)}, u32[]{:S(2)}) collective-permute-start(f32[16,1024]{1,0:T(8,128)S(1)} %get-tuple-element.29), channel_id=1, source_target_pairs={{0,256},{256,0},{1,257},{257,1},{2,258},{258,2},{3,259},{259,3},{4... | collective-permute-start | bytes 196616 | tf_op jit(solution)/shard_map/ppermute | solution.py:158
  63.3 4.2 %collective-permute-done.5.away_ref = f32[16,1024]{1,0:T(8,128)S(1)} collective-permute-done((f32[16,1024]{1,0:T(8,128)S(1)}, f32[16,1024]{1,0:T(8,128)S(1)}, u32[]{:S(2)}, u32[]{:S(2)}) %collective-permute-start.5) | collective-permute-done | bytes 65568 | tf_op jit(solution)/shard_map/ppermute | solution.py:158
  67.6 3.9 %all-to-all-done.1.parts_ref = f32[8,64,128]{2,1,0:T(8,128)S(1)} async-done(((f32[8,64,128]{2,1,0:T(8,128)}), f32[8,64,128]{2,1,0:T(8,128)S(1)}, u32[]{:S(2)}, u32[]{:S(2)}) %all-to-all-start.1) | async-done | bytes 262176 | tf_op jit(solution)/shard_map/all_to_all | solution.py:155
  71.5 0.7 sum_z.1
Async XLA Ops:
  0.6 18.3 %collective-permute-start.3 = (bf16[1024,128]{1,0:T(8,128)(2,1)}, bf16[1024,128]{1,0:T(8,128)(2,1)S(1)}, u32[]{:S(2)}, u32[]{:S(2)}) collective-permute-start(bf16[1024,128]{1,0:T(8,128)(2,1)} %refs_0_.1), channel_id=1, source_target_pairs={{0,256},{256,0},{1,257},{257,1},{2,258},{258,2},{3,259},{259,3},{4... | collective-permute-start | bytes 786440 | tf_op jit(solution)/shard_map/ppermute | solution.py:135
  3.0 16.2 %collective-permute-start = (bf16[1024,128]{1,0:T(8,128)(2,1)}, bf16[1024,128]{1,0:T(8,128)(2,1)S(1)}, u32[]{:S(2)}, u32[]{:S(2)}) collective-permute-start(bf16[1024,128]{1,0:T(8,128)(2,1)} %refs_0_.1), channel_id=1, source_target_pairs={{0,128},{64,192},{128,0},{192,64},{1,129},{65,193},{129,1},{193,65... | collective-permute-start | bytes 786440 | tf_op jit(solution)/shard_map/ppermute | solution.py:132
  6.3 12.9 %collective-permute-start.1 = (bf16[1024,128]{1,0:T(8,128)(2,1)}, bf16[1024,128]{1,0:T(8,128)(2,1)S(1)}, u32[]{:S(2)}, u32[]{:S(2)}) collective-permute-start(bf16[1024,128]{1,0:T(8,128)(2,1)} %refs_0_.1), channel_id=1, source_target_pairs={{0,64},{64,128},{128,192},{192,0},{1,65},{65,129},{129,193},{193,1... | collective-permute-start | bytes 786440 | tf_op jit(solution)/shard_map/ppermute | solution.py:132
  12.7 9.7 %collective-permute-start.2 = (bf16[1024,128]{1,0:T(8,128)(2,1)}, bf16[1024,128]{1,0:T(8,128)(2,1)S(1)}, u32[]{:S(2)}, u32[]{:S(2)}) collective-permute-start(bf16[1024,128]{1,0:T(8,128)(2,1)} %refs_0_.1), channel_id=1, source_target_pairs={{0,192},{64,0},{128,64},{192,128},{1,193},{65,1},{129,65},{193,129... | collective-permute-start | bytes 786440 | tf_op jit(solution)/shard_map/ppermute | solution.py:132
  15.5 1.2 %copy-start = (bf16[2048,256]{1,0:T(8,128)(2,1)S(1)}, bf16[2048,256]{1,0:T(8,128)(2,1)}, u32[]{:S(2)}) copy-start(bf16[2048,256]{1,0:T(8,128)(2,1)} %eigvec_ref.1) | copy-start | bytes 3145732
  16.7 0.7 copy-start.2
  17.4 1.5 %copy-start.1 = (bf16[1024,128]{1,0:T(8,128)(2,1)S(1)}, bf16[1024,128]{1,0:T(8,128)(2,1)}, u32[]{:S(2)}) copy-start(bf16[1024,128]{1,0:T(8,128)(2,1)} %refs_0_.1) | copy-start | bytes 786436
  17.4 1.6 %copy-start.3 = (f32[1024]{0:T(1024)S(1)}, f32[1024]{0:T(1024)}, u32[]{:S(2)}) copy-start(f32[1024]{0:T(1024)} %param.5) | copy-start | bytes 12292
  22.4 4.6 %collective-permute-start.4 = (bf16[4,1024,128]{2,1,0:T(8,128)(2,1)S(1)}, bf16[4,1024,128]{2,1,0:T(8,128)(2,1)S(1)}, u32[]{:S(2)}, u32[]{:S(2)}) collective-permute-start(bf16[4,1024,128]{2,1,0:T(8,128)(2,1)S(1)} %stack.1.rows_ref), channel_id=1, source_target_pairs={{0,32},{32,0},{1,33},{33,1},{2,34},{34,2},{3,35},{35,3},{4,36},{36... | collective-permute-start | bytes 3145736 | tf_op jit(solution)/shard_map/ppermute | solution.py:145
  50.6 20.8 %all-to-all-start.1 = ((f32[8,64,128]{2,1,0:T(8,128)}), f32[8,64,128]{2,1,0:T(8,128)S(1)}, u32[]{:S(2)}, u32[]{:S(2)}) async-start(f32[8,64,128]{2,1,0:T(8,128)} %sum_y.1), calls=%async_computation.1 | async-start | bytes 524288 | tf_op jit(solution)/shard_map/all_to_all | solution.py:155
  61.4 6.2 %collective-permute-start.5 = (f32[16,1024]{1,0:T(8,128)S(1)}, f32[16,1024]{1,0:T(8,128)S(1)}, u32[]{:S(2)}, u32[]{:S(2)}) collective-permute-start(f32[16,1024]{1,0:T(8,128)S(1)} %get-tuple-element.29), channel_id=1, source_target_pairs={{0,256},{256,0},{1,257},{257,1},{2,258},{258,2},{3,259},{259,3},{4... | collective-permute-start | bytes 196616 | tf_op jit(solution)/shard_map/ppermute | solution.py:158

commit v3 on v2

--- a/solution.py
+++ b/solution.py
@@ -6,10 +6,11 @@
 from jax.sharding import Mesh, PartitionSpec as P
 
 SWAP = [(0, 1), (1, 0)]
+HIDE = 20 * 10**9
 VMEM = pl.BlockSpec(memory_space=pltpu.VMEM)
 
 
-def local(kernel, out_shape, *operands, name):
+def local(kernel, out_shape, *operands, name, flops=0):
     outs = jax.tree.map(lambda _: VMEM, out_shape)
     return pl.pallas_call(
         kernel,
@@ -17,6 +18,7 @@
         in_specs=[VMEM] * len(operands),
         out_specs=outs,
         compiler_params=pltpu.CompilerParams(vmem_limit_bytes=32 * 1024 * 1024),
+        cost_estimate=pl.CostEstimate(flops=flops, bytes_accessed=0, transcendentals=0) if flops else None,
         name=name,
     )(*operands)
 
@@ -133,17 +135,17 @@
 
     across, ahead, behind = shift(2), shift(1), shift(3)
     partner = lax.ppermute(snapshots, "yl", SWAP)
+    ordered = local(
+        ordered_kernel, shape((2, 4, 32, 128), jnp.bfloat16), time_index.reshape(16, 128), eigvec, name="ordered"
+    )
+    across, ahead, behind, ordered = lax.optimization_barrier((across, ahead, behind, ordered))
+    stacked = shape((4, rows, width), jnp.bfloat16)
+    same = local(stack_kernel, stacked, snapshots, ahead, behind, across, name="stack")
+    other = lax.ppermute(same, "core", SWAP)
     weighted = (jnp.concatenate([snapshots, partner], 1).astype(jnp.float32) * cell_weight[:, None]).astype(
         jnp.bfloat16
     )
-    ordered = local(
-        ordered_kernel, shape((2, 4, 32, 128), jnp.bfloat16), time_index.reshape(16, 128), eigvec, name="ordered"
-    )
-    across, ahead, behind, weighted, ordered = lax.optimization_barrier((across, ahead, behind, weighted, ordered))
-    stacked = shape((4, rows, width), jnp.bfloat16)
-    same = local(stack_kernel, stacked, snapshots, ahead, behind, across, name="stack")
-    other = lax.ppermute(same, "core", SWAP)
-    begun = local(gram_same_kernel, shape((4, 4, 64, 128), jnp.bfloat16), same, weighted, name="gram_same")
+    begun = local(gram_same_kernel, shape((4, 4, 64, 128), jnp.bfloat16), same, weighted, name="gram_same", flops=HIDE)
     modes = local(modes_same_kernel, shape((32, rows), jnp.float32), same, ordered, name="modes_same")
     other, begun, modes = lax.optimization_barrier((other, begun, modes))
     parts = local(

time: 72.6 us -> 70.3 us (0.968)
  the two profiles are of different devices: /device:TPU:14 before, /device:TPU:8 now
where the time goes in v3:
time: 70.3 us; the launch traced here: 69.8 us
  starting transfers between devices  30.9 us (44%)
  blocking collectives  21.6 us (31%)
  waiting for transfers between devices  9.59 us (14%)
  Pallas kernels  4.85 us (7%)
  local copies, waits for them, and re-layouts  1.93 us (3%)
  between operations  0.8 us (1%)
    all_to_all x1, blocking collectives, body(): parts = lax.all_to_all(parts, ('yl', 'yh'), 0, 0, tiled=True)  21.6 us
    ppermute x3, starting transfers between devices, shift(): return lax.ppermute(snapshots, 'x', [(i, (i + k) % 4) for i in range(4)])  12 us
    all_to_all x1, starting transfers between devices, body(): parts = lax.all_to_all(parts, 'z', 0, 0, tiled=True)  10.3 us
    pallas_call x8, Pallas kernels, local(): pl.pallas_call(kernel, out_shape=out_shape, in_specs=[VMEM] * len(operand...  4.85 us
    ppermute x1, starting transfers between devices, body(): partner = lax.ppermute(snapshots, 'yl', SWAP)  4.72 us
    ppermute x1, waiting for transfers between devices, body(): away = lax.ppermute(away, 'yl', SWAP)  4.23 us
    all_to_all x1, waiting for transfers between devices, body(): parts = lax.all_to_all(parts, 'z', 0, 0, tiled=True)  3.88 us
    unnamed x8, local copies, waits for them, and re-layouts  1.93 us
  transfers between devices with their start and end apart: 7, of which 3 were waited for; matrix products, arithmetic and copies ran while one was open for 0% of the time, Pallas kernels for 4%

profile of v3, /device:TPU:8, one launch (start us, length us, event | category | flops | bytes accessed | tf_op | source)
XLA Modules:
  0.0 69.8 jit_solution(9353674259689752021)
XLA Ops:
  0.6 4.9 %collective-permute-start = (bf16[1024,128]{1,0:T(8,128)(2,1)}, bf16[1024,128]{1,0:T(8,128)(2,1)S(1)}, u32[]{:S(2)}, u32[]{:S(2)}) collective-permute-start(bf16[1024,128]{1,0:T(8,128)(2,1)} %refs_0_.1), channel_id=1, source_target_pairs={{0,128},{64,192},{128,0},{192,64},{1,129},{65,193},{129,1},{193,65... | collective-permute-start | bytes 786440 | tf_op jit(solution)/shard_map/ppermute | solution.py:134
  5.6 2.5 %collective-permute-start.1 = (bf16[1024,128]{1,0:T(8,128)(2,1)}, bf16[1024,128]{1,0:T(8,128)(2,1)S(1)}, u32[]{:S(2)}, u32[]{:S(2)}) collective-permute-start(bf16[1024,128]{1,0:T(8,128)(2,1)} %refs_0_.1), channel_id=1, source_target_pairs={{0,64},{64,128},{128,192},{192,0},{1,65},{65,129},{129,193},{193,1... | collective-permute-start | bytes 786440 | tf_op jit(solution)/shard_map/ppermute | solution.py:134
  8.1 4.6 %collective-permute-start.2 = (bf16[1024,128]{1,0:T(8,128)(2,1)}, bf16[1024,128]{1,0:T(8,128)(2,1)S(1)}, u32[]{:S(2)}, u32[]{:S(2)}) collective-permute-start(bf16[1024,128]{1,0:T(8,128)(2,1)} %refs_0_.1), channel_id=1, source_target_pairs={{0,192},{64,0},{128,64},{192,128},{1,193},{65,1},{129,65},{193,129... | collective-permute-start | bytes 786440 | tf_op jit(solution)/shard_map/ppermute | solution.py:134
  12.6 4.7 %collective-permute-start.4 = (bf16[1024,128]{1,0:T(8,128)(2,1)}, bf16[1024,128]{1,0:T(8,128)(2,1)S(1)}, u32[]{:S(2)}, u32[]{:S(2)}) collective-permute-start(bf16[1024,128]{1,0:T(8,128)(2,1)} %refs_0_.1), channel_id=1, source_target_pairs={{0,256},{256,0},{1,257},{257,1},{2,258},{258,2},{3,259},{259,3},{4... | collective-permute-start | bytes 786440 | tf_op jit(solution)/shard_map/ppermute | solution.py:137
  17.4 0.0 copy-start
  17.4 1.2 %copy-done = bf16[2048,256]{1,0:T(8,128)(2,1)S(1)} copy-done((bf16[2048,256]{1,0:T(8,128)(2,1)S(1)}, bf16[2048,256]{1,0:T(8,128)(2,1)}, u32[]{:S(2)}) %copy-start) | copy-done | bytes 1048600
  18.6 0.0 copy-start.2
  18.6 0.7 copy-done.2
  19.3 0.0 copy-start.1
  19.3 1.5 %ordered.1.ordered_ref = bf16[2,4,32,128]{3,2,1,0:T(8,128)(2,1)S(1)} custom-call(s32[16,128]{1,0:T(8,128)S(1)} %bitcast.1, bf16[2048,256]{1,0:T(8,128)(2,1)S(1)} %copy-done), custom_call_target="tpu_custom_call" | custom-call | tf_op jit(solution)/shard_map/ordered/pallas_call | solution.py:15
  20.8 0.0 collective-permute-done.refs_3_
  20.8 0.0 collective-permute-done.1.refs_1_
  20.8 0.0 collective-permute-done.2.refs_2_
  20.9 0.0 copy-done.1
  20.9 0.1 stack.1.rows_ref
  20.9 0.0 copy-start.3
  21.0 1.9 %collective-permute-start.3 = (bf16[4,1024,128]{2,1,0:T(8,128)(2,1)S(1)}, bf16[4,1024,128]{2,1,0:T(8,128)(2,1)S(1)}, u32[]{:S(2)}, u32[]{:S(2)}) collective-permute-start(bf16[4,1024,128]{2,1,0:T(8,128)(2,1)S(1)} %stack.1.rows_ref), channel_id=1, source_target_pairs={{0,32},{32,0},{1,33},{33,1},{2,34},{34,2},{3,35},{35,3},{4,36},{36... | collective-permute-start | bytes 3145736 | tf_op jit(solution)/shard_map/ppermute | solution.py:144
  22.9 0.4 modes_same.1.begun_ref
  23.3 0.0 collective-permute-done.4
  23.3 0.0 copy-done.3
  23.3 0.2 multiply_convert_fusion.weighted_ref
  23.6 0.5 gram_same.1.begun_ref
  24.0 1.5 %collective-permute-done.3.rows_ref = bf16[4,1024,128]{2,1,0:T(8,128)(2,1)S(1)} collective-permute-done((bf16[4,1024,128]{2,1,0:T(8,128)(2,1)S(1)}, bf16[4,1024,128]{2,1,0:T(8,128)(2,1)S(1)}, u32[]{:S(2)}, u32[]{:S(2)}) %collective-permute-start.3) | collective-permute-done | bytes 1048608 | tf_op jit(solution)/shard_map/ppermute | solution.py:144
  25.5 0.5 gram_other.1
  26.0 21.6 %all_to_all.10.refs_0_ = bf16[8,4,64,128]{3,2,1,0:T(8,128)(2,1)S(1)} all-to-all(bf16[8,4,64,128]{3,2,1,0:T(8,128)(2,1)S(1)} %gram_other.1), channel_id=1, replica_groups=mesh['yl'=2,'x'=4,'core'=2,'z'=8,'yh'=4] {'yl','yh'}, dimensions={0} | all-to-all | bytes 1048576 | tf_op jit(solution)/shard_map/all_to_all | solution.py:154
  47.5 0.8 %sum_y.1 = f32[8,64,128]{2,1,0:T(8,128)} custom-call(bf16[8,4,64,128]{3,2,1,0:T(8,128)(2,1)S(1)} %all_to_all.10.refs_0_), custom_call_target="tpu_custom_call" | custom-call | tf_op jit(solution)/shard_map/sum_y/pallas_call | solution.py:15
  48.3 10.3 %all-to-all-start.1 = ((f32[8,64,128]{2,1,0:T(8,128)}), f32[8,64,128]{2,1,0:T(8,128)S(1)}, u32[]{:S(2)}, u32[]{:S(2)}) async-start(f32[8,64,128]{2,1,0:T(8,128)} %sum_y.1), calls=%async_computation.1 | async-start | bytes 524288 | tf_op jit(solution)/shard_map/all_to_all | solution.py:157
  58.6 0.4 modes_other.1
  59.1 1.9 %collective-permute-start.5 = (f32[16,1024]{1,0:T(8,128)S(1)}, f32[16,1024]{1,0:T(8,128)S(1)}, u32[]{:S(2)}, u32[]{:S(2)}) collective-permute-start(f32[16,1024]{1,0:T(8,128)S(1)} %get-tuple-element.27), channel_id=1, source_target_pairs={{0,256},{256,0},{1,257},{257,1},{2,258},{258,2},{3,259},{259,3},{4... | collective-permute-start | bytes 196616 | tf_op jit(solution)/shard_map/ppermute | solution.py:160
  61.0 4.2 %collective-permute-done.5.away_ref = f32[16,1024]{1,0:T(8,128)S(1)} collective-permute-done((f32[16,1024]{1,0:T(8,128)S(1)}, f32[16,1024]{1,0:T(8,128)S(1)}, u32[]{:S(2)}, u32[]{:S(2)}) %collective-permute-start.5) | collective-permute-done | bytes 65568 | tf_op jit(solution)/shard_map/ppermute | solution.py:160
  65.2 3.9 %all-to-all-done.1.parts_ref = f32[8,64,128]{2,1,0:T(8,128)S(1)} async-done(((f32[8,64,128]{2,1,0:T(8,128)}), f32[8,64,128]{2,1,0:T(8,128)S(1)}, u32[]{:S(2)}, u32[]{:S(2)}) %all-to-all-start.1) | async-done | bytes 262176 | tf_op jit(solution)/shard_map/all_to_all | solution.py:157
  69.1 0.7 sum_z.1
Async XLA Ops:
  0.6 20.2 %collective-permute-start = (bf16[1024,128]{1,0:T(8,128)(2,1)}, bf16[1024,128]{1,0:T(8,128)(2,1)S(1)}, u32[]{:S(2)}, u32[]{:S(2)}) collective-permute-start(bf16[1024,128]{1,0:T(8,128)(2,1)} %refs_0_.1), channel_id=1, source_target_pairs={{0,128},{64,192},{128,0},{192,64},{1,129},{65,193},{129,1},{193,65... | collective-permute-start | bytes 786440 | tf_op jit(solution)/shard_map/ppermute | solution.py:134
  5.6 15.3 %collective-permute-start.1 = (bf16[1024,128]{1,0:T(8,128)(2,1)}, bf16[1024,128]{1,0:T(8,128)(2,1)S(1)}, u32[]{:S(2)}, u32[]{:S(2)}) collective-permute-start(bf16[1024,128]{1,0:T(8,128)(2,1)} %refs_0_.1), channel_id=1, source_target_pairs={{0,64},{64,128},{128,192},{192,0},{1,65},{65,129},{129,193},{193,1... | collective-permute-start | bytes 786440 | tf_op jit(solution)/shard_map/ppermute | solution.py:134
  8.1 12.8 %collective-permute-start.2 = (bf16[1024,128]{1,0:T(8,128)(2,1)}, bf16[1024,128]{1,0:T(8,128)(2,1)S(1)}, u32[]{:S(2)}, u32[]{:S(2)}) collective-permute-start(bf16[1024,128]{1,0:T(8,128)(2,1)} %refs_0_.1), channel_id=1, source_target_pairs={{0,192},{64,0},{128,64},{192,128},{1,193},{65,1},{129,65},{193,129... | collective-permute-start | bytes 786440 | tf_op jit(solution)/shard_map/ppermute | solution.py:134
  12.6 10.7 %collective-permute-start.4 = (bf16[1024,128]{1,0:T(8,128)(2,1)}, bf16[1024,128]{1,0:T(8,128)(2,1)S(1)}, u32[]{:S(2)}, u32[]{:S(2)}) collective-permute-start(bf16[1024,128]{1,0:T(8,128)(2,1)} %refs_0_.1), channel_id=1, source_target_pairs={{0,256},{256,0},{1,257},{257,1},{2,258},{258,2},{3,259},{259,3},{4... | collective-permute-start | bytes 786440 | tf_op jit(solution)/shard_map/ppermute | solution.py:137
  17.4 1.2 %copy-start = (bf16[2048,256]{1,0:T(8,128)(2,1)S(1)}, bf16[2048,256]{1,0:T(8,128)(2,1)}, u32[]{:S(2)}) copy-start(bf16[2048,256]{1,0:T(8,128)(2,1)} %eigvec_ref.1) | copy-start | bytes 3145732
  18.6 0.7 copy-start.2
  19.3 1.6 %copy-start.1 = (bf16[1024,128]{1,0:T(8,128)(2,1)S(1)}, bf16[1024,128]{1,0:T(8,128)(2,1)}, u32[]{:S(2)}) copy-start(bf16[1024,128]{1,0:T(8,128)(2,1)} %refs_0_.1) | copy-start | bytes 786436
  20.9 2.4 %copy-start.3 = (f32[1024]{0:T(1024)S(1)}, f32[1024]{0:T(1024)}, u32[]{:S(2)}) copy-start(f32[1024]{0:T(1024)} %param.5) | copy-start | bytes 12292
  21.0 4.6 %collective-permute-start.3 = (bf16[4,1024,128]{2,1,0:T(8,128)(2,1)S(1)}, bf16[4,1024,128]{2,1,0:T(8,128)(2,1)S(1)}, u32[]{:S(2)}, u32[]{:S(2)}) collective-permute-start(bf16[4,1024,128]{2,1,0:T(8,128)(2,1)S(1)} %stack.1.rows_ref), channel_id=1, source_target_pairs={{0,32},{32,0},{1,33},{33,1},{2,34},{34,2},{3,35},{35,3},{4,36},{36... | collective-permute-start | bytes 3145736 | tf_op jit(solution)/shard_map/ppermute | solution.py:144
  48.3 20.8 %all-to-all-start.1 = ((f32[8,64,128]{2,1,0:T(8,128)}), f32[8,64,128]{2,1,0:T(8,128)S(1)}, u32[]{:S(2)}, u32[]{:S(2)}) async-start(f32[8,64,128]{2,1,0:T(8,128)} %sum_y.1), calls=%async_computation.1 | async-start | bytes 524288 | tf_op jit(solution)/shard_map/all_to_all | solution.py:157
  59.1 6.2 %collective-permute-start.5 = (f32[16,1024]{1,0:T(8,128)S(1)}, f32[16,1024]{1,0:T(8,128)S(1)}, u32[]{:S(2)}, u32[]{:S(2)}) collective-permute-start(f32[16,1024]{1,0:T(8,128)S(1)} %get-tuple-element.27), channel_id=1, source_target_pairs={{0,256},{256,0},{1,257},{257,1},{2,258},{258,2},{3,259},{259,3},{4... | collective-permute-start | bytes 196616 | tf_op jit(solution)/shard_map/ppermute | solution.py:160

commit v4 on v2

v4 whole, which is shorter than its diff:
```python
import jax
import jax.numpy as jnp
from jax import lax
from jax.experimental import pallas as pl
from jax.experimental.pallas import tpu as pltpu
from jax.sharding import Mesh, PartitionSpec as P

SWAP = [(0, 1), (1, 0)]
HIDE = 20 * 10**9
VMEM = pl.BlockSpec(memory_space=pltpu.VMEM)


def local(kernel, out_shape, *operands, name, flops=0):
    outs = jax.tree.map(lambda _: VMEM, out_shape)
    return pl.pallas_call(
        kernel,
        out_shape=out_shape,
        in_specs=[VMEM] * len(operands),
        out_specs=outs,
        compiler_params=pltpu.CompilerParams(vmem_limit_bytes=32 * 1024 * 1024),
        cost_estimate=pl.CostEstimate(flops=flops, bytes_accessed=0, transcendentals=0) if flops else None,
        name=name,
    )(*operands)


def ordered_kernel(index_ref, eigvec_ref, out_ref):
    y, x, core = lax.axis_index("yl"), lax.axis_index("x"), lax.axis_index("core")
    times, modes = eigvec_ref.shape
    row = lax.broadcasted_iota(jnp.int32, (32, modes), 0)
    column = lax.broadcasted_iota(jnp.int32, (32, modes), 1)
    wanted = (row // 16) * 128 + (x * 2 + core) * 16 + row % 16
    chosen = (column == wanted).astype(jnp.float32).astype(jnp.bfloat16)
    kept = lax.dot_general(
        chosen, eigvec_ref[...], (((1,), (1,)), ((), ())), preferred_element_type=jnp.float32
    ).astype(jnp.bfloat16)
    time = lax.broadcasted_iota(jnp.int32, (times, 128), 0)
    for x1 in range(4):
        for core1 in range(2):
            index = index_ref[pl.ds(y * 8 + x1 * 2 + core1, 1), :]
            hot = (time == index).astype(jnp.float32).astype(jnp.bfloat16)
            out_ref[core1, x1] = jnp.dot(kept, hot, preferred_element_type=jnp.float32).astype(jnp.bfloat16)


def shifts():
    x = lax.axis_index("x")
    return x, (x + 2) % 4, (x + 3) % 4, (x + 1) % 4


def stack_kernel(first_ref, second_ref, out_ref):
    out_ref[0], out_ref[1] = first_ref[...], second_ref[...]


def gram_blocks(pair_ref, weighted_ref, store):
    weighted = weighted_ref[...]
    for k in range(2):
        part = lax.dot_general(
            pair_ref[k], weighted, (((0,), (0,)), ((), ())), preferred_element_type=jnp.float32
        ).astype(jnp.bfloat16)
        for side in range(2):
            for half in range(2):
                store(k, side * 2 + half, part[half * 64 : half * 64 + 64, side * 128 : side * 128 + 128])


def gram_begin_kernel(pairs, *refs):
    *pair_refs, weighted_ref, out_ref = refs
    for pair in range(pairs):

        def store(k, corner, tile):
            out_ref[pair * 2 + k, corner] = tile

        gram_blocks(pair_refs[pair], weighted_ref, store)


def gram_end_kernel(last_ref, weighted_ref, begun_ref, out_ref):
    y, core = lax.axis_index("yl"), lax.axis_index("core")
    places = shifts()

    def store(k, corner, tile):
        y2, core1, x1 = (y, 1 - y)[corner // 2], (core, 1 - core)[k // 4], places[k % 4]
        out_ref[y2 * 8 + x1 % 2 * 4 + core1 * 2 + corner % 2, x1 // 2] = tile

    for k in range(6):
        for corner in range(4):
            store(k, corner, begun_ref[k, corner])
    gram_blocks(last_ref, weighted_ref, lambda k, corner, tile: store(6 + k, corner, tile))


def modes_kernel(one_ref, two_ref, one_other_ref, two_other_ref, ordered_ref, away_ref, stay_ref):
    core, places = lax.axis_index("core"), shifts()
    total = jnp.zeros((32, stay_ref.shape[1]), jnp.float32)
    for refs, core1 in (((one_ref, two_ref), core), ((one_other_ref, two_other_ref), 1 - core)):
        for k, x1 in enumerate(places):
            total += lax.dot_general(
                ordered_ref[core1, x1], refs[k // 2][k % 2], (((1,), (1,)), ((), ())), preferred_element_type=jnp.float32
            )
    first = lax.axis_index("yl") == 0
    stay_ref[...] = jnp.where(first, total[:16], total[16:])
    away_ref[...] = jnp.where(first, total[16:], total[:16])


def sum_kernel(scaling, parts_ref, out_ref):
    for y1 in range(2):
        for high in range(2):
            total = parts_ref[y1 * 8, high].astype(jnp.float32)
            for k in range(1, 8):
                total += parts_ref[y1 * 8 + k, high].astype(jnp.float32)
            out_ref[y1 * 2 + high] = total * scaling


def last_kernel(parts_ref, stay_ref, away_ref, gram_ref, modes_ref):
    total = parts_ref[0]
    for k in range(1, 4):
        total += parts_ref[k]
    gram_ref[...] = total
    modes_ref[...] = stay_ref[...] + away_ref[...]


def body(snapshots, cell_weight, eigvec, time_index):
    rows, width = snapshots.shape
    scaling = 1.0 / (rows * lax.axis_size("zh") * lax.axis_size("zl") * lax.axis_size("yh"))
    shape = jax.ShapeDtypeStruct

    def shift(k):
        return lax.ppermute(snapshots, "x", [(i, (i + k) % 4) for i in range(4)])

    across, ahead, behind = shift(2), shift(1), shift(3)
    partner = lax.ppermute(snapshots, "yl", SWAP)
    pair = shape((2, rows, width), jnp.bfloat16)
    one = local(stack_kernel, pair, snapshots, across, name="stack_one")
    one_other = lax.ppermute(one, "core", SWAP)
    two = local(stack_kernel, pair, ahead, behind, name="stack_two", flops=HIDE)
    two_other = lax.ppermute(two, "core", SWAP)
    weighted = (jnp.concatenate([snapshots, partner], 1).astype(jnp.float32) * cell_weight[:, None]).astype(
        jnp.bfloat16
    )
    begun = local(
        lambda *refs: gram_begin_kernel(3, *refs),
        shape((6, 4, 64, 128), jnp.bfloat16),
        one,
        two,
        one_other,
        weighted,
        name="gram_begin",
        flops=HIDE,
    )
    two_other, begun = lax.optimization_barrier((two_other, begun))
    parts = local(
        gram_end_kernel, shape((16, 2, 64, 128), jnp.bfloat16), two_other, weighted, begun, name="gram_end"
    )
    parts = lax.all_to_all(parts, ("yl", "zl", "yh"), 0, 0, tiled=True)
    parts = local(lambda *refs: sum_kernel(scaling, *refs), shape((4, 64, 128), jnp.float32), parts, name="sum_y")
    parts, one, two, one_other, two_other, time_index, eigvec = lax.optimization_barrier(
        (parts, one, two, one_other, two_other, time_index, eigvec)
    )
    parts = lax.all_to_all(parts, "zh", 0, 0, tiled=True)
    ordered = local(
        ordered_kernel, shape((2, 4, 32, 128), jnp.bfloat16), time_index.reshape(16, 128), eigvec, name="ordered"
    )
    half = shape((16, rows), jnp.float32)
    blocks = one, two, one_other, two_other
    away, stay = local(modes_kernel, [half, half], *blocks, ordered, name="mode_parts")
    away = lax.ppermute(away, "yl", SWAP)
    outs = [shape((64, 128), jnp.float32), half]
    gram, modes = local(last_kernel, outs, parts, stay, away, name="sum_z")
    return gram, modes


def solution(mesh):
    fine = Mesh(mesh.devices.reshape(2, 4, 2, 4, 2, 4), ("yl", "x", "core", "zh", "zl", "yh"))
    snap, space = ("yl", "x", "core"), ("zh", "zl", "yh")
    in_specs = (P(space, snap), P(space), P(), P())
    out_specs = (P(space, snap), P(snap, space))
    return jax.shard_map(body, mesh=fine, in_specs=in_specs, out_specs=out_specs, check_vma=False)
```

time: 72.6 us -> 69.5 us (0.957)
  the two profiles are of different devices: /device:TPU:14 before, /device:TPU:64 now
where the time goes in v4:
time: 69.5 us; the launch traced here: 69 us
  starting transfers between devices  30.3 us (44%)
  blocking collectives  25.7 us (37%)
  waiting for transfers between devices  6.3 us (9%)
  Pallas kernels  4.7 us (7%)
  local copies, waits for them, and re-layouts  1 us (1%)
  between operations  0.81 us (1%)
    all_to_all x1, blocking collectives, body(): parts = lax.all_to_all(parts, ('yl', 'zl', 'yh'), 0, 0, tiled=True)  25.7 us
    ppermute x3, starting transfers between devices, shift(): return lax.ppermute(snapshots, 'x', [(i, (i + k) % 4) for i in range(4)])  10.8 us
    all_to_all x1, starting transfers between devices, body(): parts = lax.all_to_all(parts, 'zh', 0, 0, tiled=True)  9.53 us
    pallas_call x8, Pallas kernels, local(): pl.pallas_call(kernel, out_shape=out_shape, in_specs=[VMEM] * len(operand...  4.7 us
    ppermute x1, waiting for transfers between devices, body(): away = lax.ppermute(away, 'yl', SWAP)  3.68 us
    ppermute x1, starting transfers between devices, body(): partner = lax.ppermute(snapshots, 'yl', SWAP)  3.49 us
    ppermute x1, starting transfers between devices, body(): away = lax.ppermute(away, 'yl', SWAP)  2.49 us
    ppermute x1, starting transfers between devices, body(): one_other = lax.ppermute(one, 'core', SWAP)  2.05 us
  transfers between devices with their start and end apart: 8, of which 4 were waited for; matrix products, arithmetic and copies ran while one was open for 0% of the time, Pallas kernels for 4%

profile of v4, /device:TPU:64, one launch (start us, length us, event | category | flops | bytes accessed | tf_op | source)
XLA Modules:
  0.0 69.0 jit_solution(9832903559859954240)
XLA Ops:
  0.6 4.9 %collective-permute-start.3 = (bf16[1024,128]{1,0:T(8,128)(2,1)}, bf16[1024,128]{1,0:T(8,128)(2,1)S(1)}, u32[]{:S(2)}, u32[]{:S(2)}) collective-permute-start(bf16[1024,128]{1,0:T(8,128)(2,1)} %first_ref.1), channel_id=1, source_target_pairs={{0,128},{64,192},{128,0},{192,64},{1,129},{65,193},{129,1},{193,65... | collective-permute-start | bytes 786440 | tf_op jit(solution)/shard_map/ppermute | solution.py:124
  5.6 3.1 %collective-permute-start.1 = (bf16[1024,128]{1,0:T(8,128)(2,1)}, bf16[1024,128]{1,0:T(8,128)(2,1)S(1)}, u32[]{:S(2)}, u32[]{:S(2)}) collective-permute-start(bf16[1024,128]{1,0:T(8,128)(2,1)} %first_ref.1), channel_id=1, source_target_pairs={{0,192},{64,0},{128,64},{192,128},{1,193},{65,1},{129,65},{193,129... | collective-permute-start | bytes 786440 | tf_op jit(solution)/shard_map/ppermute | solution.py:124
  8.6 2.8 %collective-permute-start = (bf16[1024,128]{1,0:T(8,128)(2,1)}, bf16[1024,128]{1,0:T(8,128)(2,1)S(1)}, u32[]{:S(2)}, u32[]{:S(2)}) collective-permute-start(bf16[1024,128]{1,0:T(8,128)(2,1)} %first_ref.1), channel_id=1, source_target_pairs={{0,64},{64,128},{128,192},{192,0},{1,65},{65,129},{129,193},{193,1... | collective-permute-start | bytes 786440 | tf_op jit(solution)/shard_map/ppermute | solution.py:124
  11.4 3.5 %collective-permute-start.5 = (bf16[1024,128]{1,0:T(8,128)(2,1)}, bf16[1024,128]{1,0:T(8,128)(2,1)S(1)}, u32[]{:S(2)}, u32[]{:S(2)}) collective-permute-start(bf16[1024,128]{1,0:T(8,128)(2,1)} %first_ref.1), channel_id=1, source_target_pairs={{0,256},{256,0},{1,257},{257,1},{2,258},{258,2},{3,259},{259,3},{4... | collective-permute-start | bytes 786440 | tf_op jit(solution)/shard_map/ppermute | solution.py:127
  14.9 0.0 collective-permute-done.3.second_ref
  14.9 0.0 copy-start.1
  15.0 1.0 %copy-done.1 = bf16[1024,128]{1,0:T(8,128)(2,1)S(1)} copy-done((bf16[1024,128]{1,0:T(8,128)(2,1)S(1)}, bf16[1024,128]{1,0:T(8,128)(2,1)}, u32[]{:S(2)}) %copy-start.1) | copy-done | bytes 262168
  16.0 0.0 copy-start.2
  16.0 0.0 copy-start.4
  16.0 2.1 %collective-permute-start.4 = (bf16[2,1024,128]{2,1,0:T(8,128)(2,1)S(1)}, bf16[2,1024,128]{2,1,0:T(8,128)(2,1)S(1)}, u32[]{:S(2)}, u32[]{:S(2)}) collective-permute-start(bf16[2,1024,128]{2,1,0:T(8,128)(2,1)S(1)} %stack_one.1.refs_0_.one_ref), channel_id=1, source_target_pairs={{0,32},{32,0},{1,33},{33,1},{2,34},{34,2},{3,35},{35,3},{4,36},{36... | collective-permute-start | bytes 1572872 | tf_op jit(solution)/shard_map/ppermute | solution.py:130
  18.1 0.0 collective-permute-done.1.second_ref
  18.1 1.4 %collective-permute-done.first_ref = bf16[1024,128]{1,0:T(8,128)(2,1)S(1)} collective-permute-done((bf16[1024,128]{1,0:T(8,128)(2,1)}, bf16[1024,128]{1,0:T(8,128)(2,1)S(1)}, u32[]{:S(2)}, u32[]{:S(2)}) %collective-permute-start) | collective-permute-done | bytes 262176 | tf_op jit(solution)/shard_map/ppermute | solution.py:124
  19.5 1.9 %collective-permute-start.2 = (bf16[2,1024,128]{2,1,0:T(8,128)(2,1)S(1)}, bf16[2,1024,128]{2,1,0:T(8,128)(2,1)S(1)}, u32[]{:S(2)}, u32[]{:S(2)}) collective-permute-start(bf16[2,1024,128]{2,1,0:T(8,128)(2,1)S(1)} %stack_two.1.refs_1_.two_ref), channel_id=1, source_target_pairs={{0,32},{32,0},{1,33},{33,1},{2,34},{34,2},{3,35},{35,3},{4,36},{36... | collective-permute-start | bytes 1572872 | tf_op jit(solution)/shard_map/ppermute | solution.py:132
  21.4 0.0 collective-permute-done.5
  21.4 0.0 copy-done.2
  21.4 0.0 copy-done.4
  21.4 0.2 multiply_convert_fusion.refs_3_.weighted_ref
  21.6 0.0 collective-permute-done.4.refs_2_.one_other_ref
  21.6 0.6 gram_begin.1.begun_ref
  22.3 1.0 %collective-permute-done.2.last_ref.two_other_ref = bf16[2,1024,128]{2,1,0:T(8,128)(2,1)S(1)} collective-permute-done((bf16[2,1024,128]{2,1,0:T(8,128)(2,1)S(1)}, bf16[2,1024,128]{2,1,0:T(8,128)(2,1)S(1)}, u32[]{:S(2)}, u32[]{:S(2)}) %collective-permute-start.2) | collective-permute-done | bytes 524320 | tf_op jit(solution)/shard_map/ppermute | solution.py:132
  23.3 0.3 gram_end.1
  23.6 0.0 copy-start
  23.6 25.7 %all_to_all.10.refs_0_ = bf16[16,2,64,128]{3,2,1,0:T(8,128)(2,1)S(1)} all-to-all(bf16[16,2,64,128]{3,2,1,0:T(8,128)(2,1)S(1)} %gram_end.1), channel_id=1, replica_groups=mesh['yl'=2,'x'=4,'core'=2,'zh'=4,'zl'=2,'yh'=4] {'yl','zl','yh'}, dimensions={0} | all-to-all | bytes 1048576 | tf_op jit(solution)/shard_map/all_to_all | solution.py:150
  49.4 0.7 %sum_y.1 = f32[4,64,128]{2,1,0:T(8,128)} custom-call(bf16[16,2,64,128]{3,2,1,0:T(8,128)(2,1)S(1)} %all_to_all.10.refs_0_), custom_call_target="tpu_custom_call" | custom-call | tf_op jit(solution)/shard_map/sum_y/pallas_call | solution.py:15
  50.1 0.0 copy-start.3
  50.1 9.5 %all-to-all-start.1 = ((f32[4,64,128]{2,1,0:T(8,128)}), f32[4,64,128]{2,1,0:T(8,128)S(1)}, u32[]{:S(2)}, u32[]{:S(2)}) async-start(f32[4,64,128]{2,1,0:T(8,128)} %sum_y.1), calls=%async_computation.1 | async-start | bytes 262144 | tf_op jit(solution)/shard_map/all_to_all | solution.py:155
  59.6 0.0 copy-done
  59.6 0.0 copy-done.3
  59.6 1.5 %ordered.1.ordered_ref = bf16[2,4,32,128]{3,2,1,0:T(8,128)(2,1)S(1)} custom-call(s32[16,128]{1,0:T(8,128)S(1)} %bitcast.1, bf16[2048,256]{1,0:T(8,128)(2,1)S(1)} %copy-done), custom_call_target="tpu_custom_call" | custom-call | tf_op jit(solution)/shard_map/ordered/pallas_call | solution.py:15
  61.2 0.8 %mode_parts.1 = (f32[16,1024]{1,0:T(8,128)S(1)}, f32[16,1024]{1,0:T(8,128)S(1)}) custom-call(bf16[2,1024,128]{2,1,0:T(8,128)(2,1)S(1)} %stack_one.1.refs_0_.one_ref, bf16[2,1024,128]{2,1,0:T(8,128)(2,1)S(1)} %stack_two.1.refs_1_.two_ref, bf16[2,1024,128]{2,1,0:T(8,128)(2,1)S(1)} %collective-permute-done.4.refs_2_.one_other_ref, ...), custom_call_target="tpu_custom_call" | custom-call | tf_op jit(solution)/shard_map/mode_parts/pallas_call | solution.py:15
  61.9 2.5 %collective-permute-start.6 = (f32[16,1024]{1,0:T(8,128)S(1)}, f32[16,1024]{1,0:T(8,128)S(1)}, u32[]{:S(2)}, u32[]{:S(2)}) collective-permute-start(f32[16,1024]{1,0:T(8,128)S(1)} %get-tuple-element.23), channel_id=1, source_target_pairs={{0,256},{256,0},{1,257},{257,1},{2,258},{258,2},{3,259},{259,3},{4... | collective-permute-start | bytes 196616 | tf_op jit(solution)/shard_map/ppermute | solution.py:162
  64.4 3.7 %collective-permute-done.6.away_ref = f32[16,1024]{1,0:T(8,128)S(1)} collective-permute-done((f32[16,1024]{1,0:T(8,128)S(1)}, f32[16,1024]{1,0:T(8,128)S(1)}, u32[]{:S(2)}, u32[]{:S(2)}) %collective-permute-start.6) | collective-permute-done | bytes 65568 | tf_op jit(solution)/shard_map/ppermute | solution.py:162
  68.1 0.2 all-to-all-done.1.parts_ref
  68.4 0.7 sum_z.1
  (2 shorter events, 0.1 us)
Async XLA Ops:
  0.6 14.3 %collective-permute-start.3 = (bf16[1024,128]{1,0:T(8,128)(2,1)}, bf16[1024,128]{1,0:T(8,128)(2,1)S(1)}, u32[]{:S(2)}, u32[]{:S(2)}) collective-permute-start(bf16[1024,128]{1,0:T(8,128)(2,1)} %first_ref.1), channel_id=1, source_target_pairs={{0,128},{64,192},{128,0},{192,64},{1,129},{65,193},{129,1},{193,65... | collective-permute-start | bytes 786440 | tf_op jit(solution)/shard_map/ppermute | solution.py:124
  5.6 12.5 %collective-permute-start.1 = (bf16[1024,128]{1,0:T(8,128)(2,1)}, bf16[1024,128]{1,0:T(8,128)(2,1)S(1)}, u32[]{:S(2)}, u32[]{:S(2)}) collective-permute-start(bf16[1024,128]{1,0:T(8,128)(2,1)} %first_ref.1), channel_id=1, source_target_pairs={{0,192},{64,0},{128,64},{192,128},{1,193},{65,1},{129,65},{193,129... | collective-permute-start | bytes 786440 | tf_op jit(solution)/shard_map/ppermute | solution.py:124
  8.6 10.8 %collective-permute-start = (bf16[1024,128]{1,0:T(8,128)(2,1)}, bf16[1024,128]{1,0:T(8,128)(2,1)S(1)}, u32[]{:S(2)}, u32[]{:S(2)}) collective-permute-start(bf16[1024,128]{1,0:T(8,128)(2,1)} %first_ref.1), channel_id=1, source_target_pairs={{0,64},{64,128},{128,192},{192,0},{1,65},{65,129},{129,193},{193,1... | collective-permute-start | bytes 786440 | tf_op jit(solution)/shard_map/ppermute | solution.py:124
  11.4 10.0 %collective-permute-start.5 = (bf16[1024,128]{1,0:T(8,128)(2,1)}, bf16[1024,128]{1,0:T(8,128)(2,1)S(1)}, u32[]{:S(2)}, u32[]{:S(2)}) collective-permute-start(bf16[1024,128]{1,0:T(8,128)(2,1)} %first_ref.1), channel_id=1, source_target_pairs={{0,256},{256,0},{1,257},{257,1},{2,258},{258,2},{3,259},{259,3},{4... | collective-permute-start | bytes 786440 | tf_op jit(solution)/shard_map/ppermute | solution.py:127
  14.9 1.0 %copy-start.1 = (bf16[1024,128]{1,0:T(8,128)(2,1)S(1)}, bf16[1024,128]{1,0:T(8,128)(2,1)}, u32[]{:S(2)}) copy-start(bf16[1024,128]{1,0:T(8,128)(2,1)} %first_ref.1) | copy-start | bytes 786436
  16.0 5.4 %copy-start.2 = (bf16[1024,128]{1,0:T(8,128)(2,1)S(1)}, bf16[1024,128]{1,0:T(8,128)(2,1)}, u32[]{:S(2)}) copy-start(bf16[1024,128]{1,0:T(8,128)(2,1)} %first_ref.1) | copy-start | bytes 786436
  16.0 5.4 %copy-start.4 = (f32[1024]{0:T(1024)S(1)}, f32[1024]{0:T(1024)}, u32[]{:S(2)}) copy-start(f32[1024]{0:T(1024)} %param.5) | copy-start | bytes 12292
  16.0 5.7 %collective-permute-start.4 = (bf16[2,1024,128]{2,1,0:T(8,128)(2,1)S(1)}, bf16[2,1024,128]{2,1,0:T(8,128)(2,1)S(1)}, u32[]{:S(2)}, u32[]{:S(2)}) collective-permute-start(bf16[2,1024,128]{2,1,0:T(8,128)(2,1)S(1)} %stack_one.1.refs_0_.one_ref), channel_id=1, source_target_pairs={{0,32},{32,0},{1,33},{33,1},{2,34},{34,2},{3,35},{35,3},{4,36},{36... | collective-permute-start | bytes 1572872 | tf_op jit(solution)/shard_map/ppermute | solution.py:130
  19.5 3.8 %collective-permute-start.2 = (bf16[2,1024,128]{2,1,0:T(8,128)(2,1)S(1)}, bf16[2,1024,128]{2,1,0:T(8,128)(2,1)S(1)}, u32[]{:S(2)}, u32[]{:S(2)}) collective-permute-start(bf16[2,1024,128]{2,1,0:T(8,128)(2,1)S(1)} %stack_two.1.refs_1_.two_ref), channel_id=1, source_target_pairs={{0,32},{32,0},{1,33},{33,1},{2,34},{34,2},{3,35},{35,3},{4,36},{36... | collective-permute-start | bytes 1572872 | tf_op jit(solution)/shard_map/ppermute | solution.py:132
  23.6 36.0 %copy-start = (bf16[2048,256]{1,0:T(8,128)(2,1)S(1)}, bf16[2048,256]{1,0:T(8,128)(2,1)}, u32[]{:S(2)}) copy-start(bf16[2048,256]{1,0:T(8,128)(2,1)} %eigvec_ref) | copy-start | bytes 3145732
  50.1 9.5 %copy-start.3 = (s32[2048]{0:T(1024)S(1)}, s32[2048]{0:T(1024)}, u32[]{:S(2)}) copy-start(s32[2048]{0:T(1024)} %param.7) | copy-start | bytes 24580
  50.1 18.3 %all-to-all-start.1 = ((f32[4,64,128]{2,1,0:T(8,128)}), f32[4,64,128]{2,1,0:T(8,128)S(1)}, u32[]{:S(2)}, u32[]{:S(2)}) async-start(f32[4,64,128]{2,1,0:T(8,128)} %sum_y.1), calls=%async_computation.1 | async-start | bytes 262144 | tf_op jit(solution)/shard_map/all_to_all | solution.py:155
  61.9 6.2 %collective-permute-start.6 = (f32[16,1024]{1,0:T(8,128)S(1)}, f32[16,1024]{1,0:T(8,128)S(1)}, u32[]{:S(2)}, u32[]{:S(2)}) collective-permute-start(f32[16,1024]{1,0:T(8,128)S(1)} %get-tuple-element.23), channel_id=1, source_target_pairs={{0,256},{256,0},{1,257},{257,1},{2,258},{258,2},{3,259},{259,3},{4... | collective-permute-start | bytes 196616 | tf_op jit(solution)/shard_map/ppermute | solution.py:162

commit v5 on v4

--- a/solution.py
+++ b/solution.py
@@ -43,7 +43,7 @@
 
 def shifts():
     x = lax.axis_index("x")
-    return x, (x + 2) % 4, (x + 3) % 4, (x + 1) % 4
+    return x, (x + 2) % 4, x + 1 - x % 2 * 2, 3 - x
 
 
 def stack_kernel(first_ref, second_ref, out_ref):
@@ -120,10 +120,10 @@
     scaling = 1.0 / (rows * lax.axis_size("zh") * lax.axis_size("zl") * lax.axis_size("yh"))
     shape = jax.ShapeDtypeStruct
 
-    def shift(k):
-        return lax.ppermute(snapshots, "x", [(i, (i + k) % 4) for i in range(4)])
+    def trade(k):
+        return lax.ppermute(snapshots, "x", [(i, i ^ k) for i in range(4)])
 
-    across, ahead, behind = shift(2), shift(1), shift(3)
+    across, ahead, behind = trade(2), trade(1), trade(3)
     partner = lax.ppermute(snapshots, "yl", SWAP)
     pair = shape((2, rows, width), jnp.bfloat16)
     one = local(stack_kernel, pair, snapshots, across, name="stack_one")

time: 69.5 us -> 68.3 us (0.983)
  starting transfers between devices: 30.3 us -> 29.4 us
    ppermute x3, starting transfers between devices: 10.8 us -> 9.91 us  [trade(): return lax.ppermute(snapshots, 'x', [(i, i ^ k) for i in range(4)])]
  transfers between devices with their start and end apart: 8 -> 8, of which waited for: 4 -> 5; matrix products, arithmetic and copies ran while one was open for 0% -> 0% of each run, Pallas kernels for 4% -> 4%
where the time goes in v5:
time: 68.3 us; the launch traced here: 67.8 us
  starting transfers between devices  29.4 us (43%)
  blocking collectives  25.7 us (38%)
  waiting for transfers between devices  5.97 us (9%)
  Pallas kernels  4.7 us (7%)
  local copies, waits for them, and re-layouts  1 us (1%)
  between operations  0.8 us (1%)
    all_to_all x1, blocking collectives, body(): parts = lax.all_to_all(parts, ('yl', 'zl', 'yh'), 0, 0, tiled=True)  25.7 us
    ppermute x3, starting transfers between devices, trade(): return lax.ppermute(snapshots, 'x', [(i, i ^ k) for i in range(4)])  9.91 us
    all_to_all x1, starting transfers between devices, body(): parts = lax.all_to_all(parts, 'zh', 0, 0, tiled=True)  9.53 us
    pallas_call x8, Pallas kernels, local(): pl.pallas_call(kernel, out_shape=out_shape, in_specs=[VMEM] * len(operand...  4.7 us
    ppermute x1, waiting for transfers between devices, body(): away = lax.ppermute(away, 'yl', SWAP)  3.68 us
    ppermute x1, starting transfers between devices, body(): partner = lax.ppermute(snapshots, 'yl', SWAP)  3.49 us
    ppermute x1, starting transfers between devices, body(): away = lax.ppermute(away, 'yl', SWAP)  2.49 us
    ppermute x1, starting transfers between devices, body(): one_other = lax.ppermute(one, 'core', SWAP)  2.05 us
  transfers between devices with their start and end apart: 8, of which 5 were waited for; matrix products, arithmetic and copies ran while one was open for 0% of the time, Pallas kernels for 4%

profile of v5, /device:TPU:64, one launch (start us, length us, event | category | flops | bytes accessed | tf_op | source)
XLA Modules:
  0.0 67.8 jit_solution(18118082023063106548)
XLA Ops:
  0.6 4.9 %collective-permute-start.3 = (bf16[1024,128]{1,0:T(8,128)(2,1)}, bf16[1024,128]{1,0:T(8,128)(2,1)S(1)}, u32[]{:S(2)}, u32[]{:S(2)}) collective-permute-start(bf16[1024,128]{1,0:T(8,128)(2,1)} %first_ref.1), channel_id=1, source_target_pairs={{0,128},{64,192},{128,0},{192,64},{1,129},{65,193},{129,1},{193,65... | collective-permute-start | bytes 786440 | tf_op jit(solution)/shard_map/ppermute | solution.py:124
  5.6 3.1 %collective-permute-start.1 = (bf16[1024,128]{1,0:T(8,128)(2,1)}, bf16[1024,128]{1,0:T(8,128)(2,1)S(1)}, u32[]{:S(2)}, u32[]{:S(2)}) collective-permute-start(bf16[1024,128]{1,0:T(8,128)(2,1)} %first_ref.1), channel_id=1, source_target_pairs={{0,192},{64,128},{128,64},{192,0},{1,193},{65,129},{129,65},{193,1... | collective-permute-start | bytes 786440 | tf_op jit(solution)/shard_map/ppermute | solution.py:124
  8.6 1.9 %collective-permute-start = (bf16[1024,128]{1,0:T(8,128)(2,1)}, bf16[1024,128]{1,0:T(8,128)(2,1)S(1)}, u32[]{:S(2)}, u32[]{:S(2)}) collective-permute-start(bf16[1024,128]{1,0:T(8,128)(2,1)} %first_ref.1), channel_id=1, source_target_pairs={{0,64},{64,0},{128,192},{192,128},{1,65},{65,1},{129,193},{193,129... | collective-permute-start | bytes 786440 | tf_op jit(solution)/shard_map/ppermute | solution.py:124
  10.6 3.5 %collective-permute-start.5 = (bf16[1024,128]{1,0:T(8,128)(2,1)}, bf16[1024,128]{1,0:T(8,128)(2,1)S(1)}, u32[]{:S(2)}, u32[]{:S(2)}) collective-permute-start(bf16[1024,128]{1,0:T(8,128)(2,1)} %first_ref.1), channel_id=1, source_target_pairs={{0,256},{256,0},{1,257},{257,1},{2,258},{258,2},{3,259},{259,3},{4... | collective-permute-start | bytes 786440 | tf_op jit(solution)/shard_map/ppermute | solution.py:127
  14.1 0.0 collective-permute-done.3.second_ref
  14.1 0.0 copy-start.1
  14.1 1.0 %copy-done.1 = bf16[1024,128]{1,0:T(8,128)(2,1)S(1)} copy-done((bf16[1024,128]{1,0:T(8,128)(2,1)S(1)}, bf16[1024,128]{1,0:T(8,128)(2,1)}, u32[]{:S(2)}) %copy-start.1) | copy-done | bytes 262168
  15.1 0.0 copy-start.2
  15.1 0.0 copy-start.4
  15.1 2.1 %collective-permute-start.4 = (bf16[2,1024,128]{2,1,0:T(8,128)(2,1)S(1)}, bf16[2,1024,128]{2,1,0:T(8,128)(2,1)S(1)}, u32[]{:S(2)}, u32[]{:S(2)}) collective-permute-start(bf16[2,1024,128]{2,1,0:T(8,128)(2,1)S(1)} %stack_one.1.refs_0_.one_ref), channel_id=1, source_target_pairs={{0,32},{32,0},{1,33},{33,1},{2,34},{34,2},{3,35},{35,3},{4,36},{36... | collective-permute-start | bytes 1572872 | tf_op jit(solution)/shard_map/ppermute | solution.py:130
  17.2 0.7 %collective-permute-done.1.second_ref = bf16[1024,128]{1,0:T(8,128)(2,1)S(1)} collective-permute-done((bf16[1024,128]{1,0:T(8,128)(2,1)}, bf16[1024,128]{1,0:T(8,128)(2,1)S(1)}, u32[]{:S(2)}, u32[]{:S(2)}) %collective-permute-start.1) | collective-permute-done | bytes 262176 | tf_op jit(solution)/shard_map/ppermute | solution.py:124
  17.9 0.3 collective-permute-done.first_ref
  18.3 1.9 %collective-permute-start.2 = (bf16[2,1024,128]{2,1,0:T(8,128)(2,1)S(1)}, bf16[2,1024,128]{2,1,0:T(8,128)(2,1)S(1)}, u32[]{:S(2)}, u32[]{:S(2)}) collective-permute-start(bf16[2,1024,128]{2,1,0:T(8,128)(2,1)S(1)} %stack_two.1.refs_1_.two_ref), channel_id=1, source_target_pairs={{0,32},{32,0},{1,33},{33,1},{2,34},{34,2},{3,35},{35,3},{4,36},{36... | collective-permute-start | bytes 1572872 | tf_op jit(solution)/shard_map/ppermute | solution.py:132
  20.2 0.0 collective-permute-done.5
  20.2 0.0 copy-done.2
  20.2 0.0 copy-done.4
  20.2 0.2 multiply_convert_fusion.refs_3_.weighted_ref
  20.4 0.0 collective-permute-done.4.refs_2_.one_other_ref
  20.4 0.6 gram_begin.1.begun_ref
  21.1 1.0 %collective-permute-done.2.last_ref.two_other_ref = bf16[2,1024,128]{2,1,0:T(8,128)(2,1)S(1)} collective-permute-done((bf16[2,1024,128]{2,1,0:T(8,128)(2,1)S(1)}, bf16[2,1024,128]{2,1,0:T(8,128)(2,1)S(1)}, u32[]{:S(2)}, u32[]{:S(2)}) %collective-permute-start.2) | collective-permute-done | bytes 524320 | tf_op jit(solution)/shard_map/ppermute | solution.py:132
  22.1 0.3 gram_end.1
  22.4 0.0 copy-start
  22.4 25.7 %all_to_all.10.refs_0_ = bf16[16,2,64,128]{3,2,1,0:T(8,128)(2,1)S(1)} all-to-all(bf16[16,2,64,128]{3,2,1,0:T(8,128)(2,1)S(1)} %gram_end.1), channel_id=1, replica_groups=mesh['yl'=2,'x'=4,'core'=2,'zh'=4,'zl'=2,'yh'=4] {'yl','zl','yh'}, dimensions={0} | all-to-all | bytes 1048576 | tf_op jit(solution)/shard_map/all_to_all | solution.py:150
  48.2 0.7 %sum_y.1 = f32[4,64,128]{2,1,0:T(8,128)} custom-call(bf16[16,2,64,128]{3,2,1,0:T(8,128)(2,1)S(1)} %all_to_all.10.refs_0_), custom_call_target="tpu_custom_call" | custom-call | tf_op jit(solution)/shard_map/sum_y/pallas_call | solution.py:15
  48.9 0.0 copy-start.3
  48.9 9.5 %all-to-all-start.1 = ((f32[4,64,128]{2,1,0:T(8,128)}), f32[4,64,128]{2,1,0:T(8,128)S(1)}, u32[]{:S(2)}, u32[]{:S(2)}) async-start(f32[4,64,128]{2,1,0:T(8,128)} %sum_y.1), calls=%async_computation.1 | async-start | bytes 262144 | tf_op jit(solution)/shard_map/all_to_all | solution.py:155
  58.4 0.0 copy-done
  58.4 0.0 copy-done.3
  58.4 1.5 %ordered.1.ordered_ref = bf16[2,4,32,128]{3,2,1,0:T(8,128)(2,1)S(1)} custom-call(s32[16,128]{1,0:T(8,128)S(1)} %bitcast.1, bf16[2048,256]{1,0:T(8,128)(2,1)S(1)} %copy-done), custom_call_target="tpu_custom_call" | custom-call | tf_op jit(solution)/shard_map/ordered/pallas_call | solution.py:15
  59.9 0.8 %mode_parts.1 = (f32[16,1024]{1,0:T(8,128)S(1)}, f32[16,1024]{1,0:T(8,128)S(1)}) custom-call(bf16[2,1024,128]{2,1,0:T(8,128)(2,1)S(1)} %stack_one.1.refs_0_.one_ref, bf16[2,1024,128]{2,1,0:T(8,128)(2,1)S(1)} %stack_two.1.refs_1_.two_ref, bf16[2,1024,128]{2,1,0:T(8,128)(2,1)S(1)} %collective-permute-done.4.refs_2_.one_other_ref, ...), custom_call_target="tpu_custom_call" | custom-call | tf_op jit(solution)/shard_map/mode_parts/pallas_call | solution.py:15
  60.7 2.5 %collective-permute-start.6 = (f32[16,1024]{1,0:T(8,128)S(1)}, f32[16,1024]{1,0:T(8,128)S(1)}, u32[]{:S(2)}, u32[]{:S(2)}) collective-permute-start(f32[16,1024]{1,0:T(8,128)S(1)} %get-tuple-element.23), channel_id=1, source_target_pairs={{0,256},{256,0},{1,257},{257,1},{2,258},{258,2},{3,259},{259,3},{4... | collective-permute-start | bytes 196616 | tf_op jit(solution)/shard_map/ppermute | solution.py:162
  63.2 3.7 %collective-permute-done.6.away_ref = f32[16,1024]{1,0:T(8,128)S(1)} collective-permute-done((f32[16,1024]{1,0:T(8,128)S(1)}, f32[16,1024]{1,0:T(8,128)S(1)}, u32[]{:S(2)}, u32[]{:S(2)}) %collective-permute-start.6) | collective-permute-done | bytes 65568 | tf_op jit(solution)/shard_map/ppermute | solution.py:162
  66.9 0.2 all-to-all-done.1.parts_ref
  67.1 0.7 sum_z.1
  (2 shorter events, 0.1 us)
Async XLA Ops:
  0.6 13.4 %collective-permute-start.3 = (bf16[1024,128]{1,0:T(8,128)(2,1)}, bf16[1024,128]{1,0:T(8,128)(2,1)S(1)}, u32[]{:S(2)}, u32[]{:S(2)}) collective-permute-start(bf16[1024,128]{1,0:T(8,128)(2,1)} %first_ref.1), channel_id=1, source_target_pairs={{0,128},{64,192},{128,0},{192,64},{1,129},{65,193},{129,1},{193,65... | collective-permute-start | bytes 786440 | tf_op jit(solution)/shard_map/ppermute | solution.py:124
  5.6 12.3 %collective-permute-start.1 = (bf16[1024,128]{1,0:T(8,128)(2,1)}, bf16[1024,128]{1,0:T(8,128)(2,1)S(1)}, u32[]{:S(2)}, u32[]{:S(2)}) collective-permute-start(bf16[1024,128]{1,0:T(8,128)(2,1)} %first_ref.1), channel_id=1, source_target_pairs={{0,192},{64,128},{128,64},{192,0},{1,193},{65,129},{129,65},{193,1... | collective-permute-start | bytes 786440 | tf_op jit(solution)/shard_map/ppermute | solution.py:124
  8.6 9.6 %collective-permute-start = (bf16[1024,128]{1,0:T(8,128)(2,1)}, bf16[1024,128]{1,0:T(8,128)(2,1)S(1)}, u32[]{:S(2)}, u32[]{:S(2)}) collective-permute-start(bf16[1024,128]{1,0:T(8,128)(2,1)} %first_ref.1), channel_id=1, source_target_pairs={{0,64},{64,0},{128,192},{192,128},{1,65},{65,1},{129,193},{193,129... | collective-permute-start | bytes 786440 | tf_op jit(solution)/shard_map/ppermute | solution.py:124
  10.6 9.6 %collective-permute-start.5 = (bf16[1024,128]{1,0:T(8,128)(2,1)}, bf16[1024,128]{1,0:T(8,128)(2,1)S(1)}, u32[]{:S(2)}, u32[]{:S(2)}) collective-permute-start(bf16[1024,128]{1,0:T(8,128)(2,1)} %first_ref.1), channel_id=1, source_target_pairs={{0,256},{256,0},{1,257},{257,1},{2,258},{258,2},{3,259},{259,3},{4... | collective-permute-start | bytes 786440 | tf_op jit(solution)/shard_map/ppermute | solution.py:127
  14.1 1.0 %copy-start.1 = (bf16[1024,128]{1,0:T(8,128)(2,1)S(1)}, bf16[1024,128]{1,0:T(8,128)(2,1)}, u32[]{:S(2)}) copy-start(bf16[1024,128]{1,0:T(8,128)(2,1)} %first_ref.1) | copy-start | bytes 786436
  15.1 5.1 %copy-start.2 = (bf16[1024,128]{1,0:T(8,128)(2,1)S(1)}, bf16[1024,128]{1,0:T(8,128)(2,1)}, u32[]{:S(2)}) copy-start(bf16[1024,128]{1,0:T(8,128)(2,1)} %first_ref.1) | copy-start | bytes 786436
  15.1 5.1 %copy-start.4 = (f32[1024]{0:T(1024)S(1)}, f32[1024]{0:T(1024)}, u32[]{:S(2)}) copy-start(f32[1024]{0:T(1024)} %param.5) | copy-start | bytes 12292
  15.1 5.3 %collective-permute-start.4 = (bf16[2,1024,128]{2,1,0:T(8,128)(2,1)S(1)}, bf16[2,1024,128]{2,1,0:T(8,128)(2,1)S(1)}, u32[]{:S(2)}, u32[]{:S(2)}) collective-permute-start(bf16[2,1024,128]{2,1,0:T(8,128)(2,1)S(1)} %stack_one.1.refs_0_.one_ref), channel_id=1, source_target_pairs={{0,32},{32,0},{1,33},{33,1},{2,34},{34,2},{3,35},{35,3},{4,36},{36... | collective-permute-start | bytes 1572872 | tf_op jit(solution)/shard_map/ppermute | solution.py:130
  18.3 3.8 %collective-permute-start.2 = (bf16[2,1024,128]{2,1,0:T(8,128)(2,1)S(1)}, bf16[2,1024,128]{2,1,0:T(8,128)(2,1)S(1)}, u32[]{:S(2)}, u32[]{:S(2)}) collective-permute-start(bf16[2,1024,128]{2,1,0:T(8,128)(2,1)S(1)} %stack_two.1.refs_1_.two_ref), channel_id=1, source_target_pairs={{0,32},{32,0},{1,33},{33,1},{2,34},{34,2},{3,35},{35,3},{4,36},{36... | collective-permute-start | bytes 1572872 | tf_op jit(solution)/shard_map/ppermute | solution.py:132
  22.4 36.0 %copy-start = (bf16[2048,256]{1,0:T(8,128)(2,1)S(1)}, bf16[2048,256]{1,0:T(8,128)(2,1)}, u32[]{:S(2)}) copy-start(bf16[2048,256]{1,0:T(8,128)(2,1)} %eigvec_ref) | copy-start | bytes 3145732
  48.9 9.5 %copy-start.3 = (s32[2048]{0:T(1024)S(1)}, s32[2048]{0:T(1024)}, u32[]{:S(2)}) copy-start(s32[2048]{0:T(1024)} %param.7) | copy-start | bytes 24580
  48.9 18.3 %all-to-all-start.1 = ((f32[4,64,128]{2,1,0:T(8,128)}), f32[4,64,128]{2,1,0:T(8,128)S(1)}, u32[]{:S(2)}, u32[]{:S(2)}) async-start(f32[4,64,128]{2,1,0:T(8,128)} %sum_y.1), calls=%async_computation.1 | async-start | bytes 262144 | tf_op jit(solution)/shard_map/all_to_all | solution.py:155
  60.7 6.2 %collective-permute-start.6 = (f32[16,1024]{1,0:T(8,128)S(1)}, f32[16,1024]{1,0:T(8,128)S(1)}, u32[]{:S(2)}, u32[]{:S(2)}) collective-permute-start(f32[16,1024]{1,0:T(8,128)S(1)} %get-tuple-element.23), channel_id=1, source_target_pairs={{0,256},{256,0},{1,257},{257,1},{2,258},{258,2},{3,259},{259,3},{4... | collective-permute-start | bytes 196616 | tf_op jit(solution)/shard_map/ppermute | solution.py:162

commit v6 on v5

--- a/solution.py
+++ b/solution.py
@@ -77,7 +77,7 @@
 
     def store(k, corner, tile):
         y2, core1, x1 = (y, 1 - y)[corner // 2], (core, 1 - core)[k // 4], places[k % 4]
-        out_ref[y2 * 8 + x1 % 2 * 4 + core1 * 2 + corner % 2, x1 // 2] = tile
+        out_ref[(core1 * 2 + corner % 2) * 4 + x1 % 2 * 2 + y2, x1 // 2] = tile
 
     for k in range(6):
         for corner in range(4):
@@ -101,9 +101,9 @@
 def sum_kernel(scaling, parts_ref, out_ref):
     for y1 in range(2):
         for high in range(2):
-            total = parts_ref[y1 * 8, high].astype(jnp.float32)
+            total = parts_ref[y1, high].astype(jnp.float32)
             for k in range(1, 8):
-                total += parts_ref[y1 * 8 + k, high].astype(jnp.float32)
+                total += parts_ref[k * 2 + y1, high].astype(jnp.float32)
             out_ref[y1 * 2 + high] = total * scaling
 
 
@@ -147,7 +147,7 @@
     parts = local(
         gram_end_kernel, shape((16, 2, 64, 128), jnp.bfloat16), two_other, weighted, begun, name="gram_end"
     )
-    parts = lax.all_to_all(parts, ("yl", "zl", "yh"), 0, 0, tiled=True)
+    parts = lax.all_to_all(parts, ("yh", "zl", "yl"), 0, 0, tiled=True)
     parts = local(lambda *refs: sum_kernel(scaling, *refs), shape((4, 64, 128), jnp.float32), parts, name="sum_y")
     parts, one, two, one_other, two_other, time_index, eigvec = lax.optimization_barrier(
         (parts, one, two, one_other, two_other, time_index, eigvec)

time: 68.3 us -> 67.5 us (0.988)
  the two profiles are of different devices: /device:TPU:64 before, /device:TPU:8 now
where the time goes in v6:
time: 67.5 us; the launch traced here: 67 us
  starting transfers between devices  33.9 us (50%)
  blocking collectives  21.9 us (32%)
  Pallas kernels  4.7 us (7%)
  waiting for transfers between devices  4.47 us (7%)
  local copies, waits for them, and re-layouts  1 us (1%)
  between operations  0.82 us (1%)
    all_to_all x1, blocking collectives, body(): parts = lax.all_to_all(parts, ('yh', 'zl', 'yl'), 0, 0, tiled=True)  21.9 us
    ppermute x3, starting transfers between devices, trade(): return lax.ppermute(snapshots, 'x', [(i, i ^ k) for i in range(4)])  9.91 us
    all_to_all x1, starting transfers between devices, body(): parts = lax.all_to_all(parts, 'zh', 0, 0, tiled=True)  9.53 us
    ppermute x1, starting transfers between devices, body(): partner = lax.ppermute(snapshots, 'yl', SWAP)  7.05 us
    pallas_call x8, Pallas kernels, local(): pl.pallas_call(kernel, out_shape=out_shape, in_specs=[VMEM] * len(operand...  4.7 us
    ppermute x1, waiting for transfers between devices, body(): away = lax.ppermute(away, 'yl', SWAP)  3.22 us
    ppermute x1, starting transfers between devices, body(): away = lax.ppermute(away, 'yl', SWAP)  2.95 us
    ppermute x1, starting transfers between devices, body(): two_other = lax.ppermute(two, 'core', SWAP)  2.41 us
  transfers between devices with their start and end apart: 8, of which 3 were waited for; matrix products, arithmetic and copies ran while one was open for 0% of the time, Pallas kernels for 4%

profile of v6, /device:TPU:8, one launch (start us, length us, event | category | flops | bytes accessed | tf_op | source)
XLA Modules:
  0.0 67.0 jit_solution(1065902640424080940)
XLA Ops:
  0.6 4.9 %collective-permute-start.3 = (bf16[1024,128]{1,0:T(8,128)(2,1)}, bf16[1024,128]{1,0:T(8,128)(2,1)S(1)}, u32[]{:S(2)}, u32[]{:S(2)}) collective-permute-start(bf16[1024,128]{1,0:T(8,128)(2,1)} %first_ref.1), channel_id=1, source_target_pairs={{0,128},{64,192},{128,0},{192,64},{1,129},{65,193},{129,1},{193,65... | collective-permute-start | bytes 786440 | tf_op jit(solution)/shard_map/ppermute | solution.py:124
  5.6 3.1 %collective-permute-start.1 = (bf16[1024,128]{1,0:T(8,128)(2,1)}, bf16[1024,128]{1,0:T(8,128)(2,1)S(1)}, u32[]{:S(2)}, u32[]{:S(2)}) collective-permute-start(bf16[1024,128]{1,0:T(8,128)(2,1)} %first_ref.1), channel_id=1, source_target_pairs={{0,192},{64,128},{128,64},{192,0},{1,193},{65,129},{129,65},{193,1... | collective-permute-start | bytes 786440 | tf_op jit(solution)/shard_map/ppermute | solution.py:124
  8.6 1.9 %collective-permute-start = (bf16[1024,128]{1,0:T(8,128)(2,1)}, bf16[1024,128]{1,0:T(8,128)(2,1)S(1)}, u32[]{:S(2)}, u32[]{:S(2)}) collective-permute-start(bf16[1024,128]{1,0:T(8,128)(2,1)} %first_ref.1), channel_id=1, source_target_pairs={{0,64},{64,0},{128,192},{192,128},{1,65},{65,1},{129,193},{193,129... | collective-permute-start | bytes 786440 | tf_op jit(solution)/shard_map/ppermute | solution.py:124
  10.6 7.0 %collective-permute-start.5 = (bf16[1024,128]{1,0:T(8,128)(2,1)}, bf16[1024,128]{1,0:T(8,128)(2,1)S(1)}, u32[]{:S(2)}, u32[]{:S(2)}) collective-permute-start(bf16[1024,128]{1,0:T(8,128)(2,1)} %first_ref.1), channel_id=1, source_target_pairs={{0,256},{256,0},{1,257},{257,1},{2,258},{258,2},{3,259},{259,3},{4... | collective-permute-start | bytes 786440 | tf_op jit(solution)/shard_map/ppermute | solution.py:127
  17.6 0.0 collective-permute-done.3.second_ref
  17.6 0.0 copy-start.1
  17.6 1.0 %copy-done.1 = bf16[1024,128]{1,0:T(8,128)(2,1)S(1)} copy-done((bf16[1024,128]{1,0:T(8,128)(2,1)S(1)}, bf16[1024,128]{1,0:T(8,128)(2,1)}, u32[]{:S(2)}) %copy-start.1) | copy-done | bytes 262168
  18.7 0.0 copy-start.2
  18.7 0.0 copy-start.4
  18.7 2.1 %collective-permute-start.4 = (bf16[2,1024,128]{2,1,0:T(8,128)(2,1)S(1)}, bf16[2,1024,128]{2,1,0:T(8,128)(2,1)S(1)}, u32[]{:S(2)}, u32[]{:S(2)}) collective-permute-start(bf16[2,1024,128]{2,1,0:T(8,128)(2,1)S(1)} %stack_one.1.refs_0_.one_ref), channel_id=1, source_target_pairs={{0,32},{32,0},{1,33},{33,1},{2,34},{34,2},{3,35},{35,3},{4,36},{36... | collective-permute-start | bytes 1572872 | tf_op jit(solution)/shard_map/ppermute | solution.py:130
  20.7 0.0 collective-permute-done.1.second_ref
  20.7 0.0 collective-permute-done.first_ref
  20.8 2.4 %collective-permute-start.2 = (bf16[2,1024,128]{2,1,0:T(8,128)(2,1)S(1)}, bf16[2,1024,128]{2,1,0:T(8,128)(2,1)S(1)}, u32[]{:S(2)}, u32[]{:S(2)}) collective-permute-start(bf16[2,1024,128]{2,1,0:T(8,128)(2,1)S(1)} %stack_two.1.refs_1_.two_ref), channel_id=1, source_target_pairs={{0,32},{32,0},{1,33},{33,1},{2,34},{34,2},{3,35},{35,3},{4,36},{36... | collective-permute-start | bytes 1572872 | tf_op jit(solution)/shard_map/ppermute | solution.py:132
  23.2 0.0 collective-permute-done.5
  23.2 0.0 copy-done.2
  23.2 0.0 copy-done.4
  23.2 0.2 multiply_convert_fusion.refs_3_.weighted_ref
  23.5 0.0 collective-permute-done.4.refs_2_.one_other_ref
  23.5 0.6 gram_begin.1.begun_ref
  24.1 0.6 collective-permute-done.2.last_ref.two_other_ref
  24.7 0.3 gram_end.1
  25.1 0.0 copy-start
  25.1 21.9 %all_to_all.10.refs_0_ = bf16[16,2,64,128]{3,2,1,0:T(8,128)(2,1)S(1)} all-to-all(bf16[16,2,64,128]{3,2,1,0:T(8,128)(2,1)S(1)} %gram_end.1), channel_id=1, replica_groups=mesh['yl'=2,'x'=4,'core'=2,'zh'=4,'zl'=2,'yh'=4] {'yh','zl','yl'}, dimensions={0} | all-to-all | bytes 1048576 | tf_op jit(solution)/shard_map/all_to_all | solution.py:150
  47.0 0.7 %sum_y.1 = f32[4,64,128]{2,1,0:T(8,128)} custom-call(bf16[16,2,64,128]{3,2,1,0:T(8,128)(2,1)S(1)} %all_to_all.10.refs_0_), custom_call_target="tpu_custom_call" | custom-call | tf_op jit(solution)/shard_map/sum_y/pallas_call | solution.py:15
  47.7 0.0 copy-start.3
  47.7 9.5 %all-to-all-start.1 = ((f32[4,64,128]{2,1,0:T(8,128)}), f32[4,64,128]{2,1,0:T(8,128)S(1)}, u32[]{:S(2)}, u32[]{:S(2)}) async-start(f32[4,64,128]{2,1,0:T(8,128)} %sum_y.1), calls=%async_computation.1 | async-start | bytes 262144 | tf_op jit(solution)/shard_map/all_to_all | solution.py:155
  57.2 0.0 copy-done
  57.2 0.0 copy-done.3
  57.2 1.5 %ordered.1.ordered_ref = bf16[2,4,32,128]{3,2,1,0:T(8,128)(2,1)S(1)} custom-call(s32[16,128]{1,0:T(8,128)S(1)} %bitcast.1, bf16[2048,256]{1,0:T(8,128)(2,1)S(1)} %copy-done), custom_call_target="tpu_custom_call" | custom-call | tf_op jit(solution)/shard_map/ordered/pallas_call | solution.py:15
  58.8 0.8 %mode_parts.1 = (f32[16,1024]{1,0:T(8,128)S(1)}, f32[16,1024]{1,0:T(8,128)S(1)}) custom-call(bf16[2,1024,128]{2,1,0:T(8,128)(2,1)S(1)} %stack_one.1.refs_0_.one_ref, bf16[2,1024,128]{2,1,0:T(8,128)(2,1)S(1)} %stack_two.1.refs_1_.two_ref, bf16[2,1024,128]{2,1,0:T(8,128)(2,1)S(1)} %collective-permute-done.4.refs_2_.one_other_ref, ...), custom_call_target="tpu_custom_call" | custom-call | tf_op jit(solution)/shard_map/mode_parts/pallas_call | solution.py:15
  59.5 2.9 %collective-permute-start.6 = (f32[16,1024]{1,0:T(8,128)S(1)}, f32[16,1024]{1,0:T(8,128)S(1)}, u32[]{:S(2)}, u32[]{:S(2)}) collective-permute-start(f32[16,1024]{1,0:T(8,128)S(1)} %get-tuple-element.23), channel_id=1, source_target_pairs={{0,256},{256,0},{1,257},{257,1},{2,258},{258,2},{3,259},{259,3},{4... | collective-permute-start | bytes 196616 | tf_op jit(solution)/shard_map/ppermute | solution.py:162
  62.5 3.2 %collective-permute-done.6.away_ref = f32[16,1024]{1,0:T(8,128)S(1)} collective-permute-done((f32[16,1024]{1,0:T(8,128)S(1)}, f32[16,1024]{1,0:T(8,128)S(1)}, u32[]{:S(2)}, u32[]{:S(2)}) %collective-permute-start.6) | collective-permute-done | bytes 65568 | tf_op jit(solution)/shard_map/ppermute | solution.py:162
  65.7 0.6 all-to-all-done.1.parts_ref
  66.3 0.7 sum_z.1
  (2 shorter events, 0.1 us)
Async XLA Ops:
  0.6 17.0 %collective-permute-start.3 = (bf16[1024,128]{1,0:T(8,128)(2,1)}, bf16[1024,128]{1,0:T(8,128)(2,1)S(1)}, u32[]{:S(2)}, u32[]{:S(2)}) collective-permute-start(bf16[1024,128]{1,0:T(8,128)(2,1)} %first_ref.1), channel_id=1, source_target_pairs={{0,128},{64,192},{128,0},{192,64},{1,129},{65,193},{129,1},{193,65... | collective-permute-start | bytes 786440 | tf_op jit(solution)/shard_map/ppermute | solution.py:124
  5.6 15.2 %collective-permute-start.1 = (bf16[1024,128]{1,0:T(8,128)(2,1)}, bf16[1024,128]{1,0:T(8,128)(2,1)S(1)}, u32[]{:S(2)}, u32[]{:S(2)}) collective-permute-start(bf16[1024,128]{1,0:T(8,128)(2,1)} %first_ref.1), channel_id=1, source_target_pairs={{0,192},{64,128},{128,64},{192,0},{1,193},{65,129},{129,65},{193,1... | collective-permute-start | bytes 786440 | tf_op jit(solution)/shard_map/ppermute | solution.py:124
  8.6 12.1 %collective-permute-start = (bf16[1024,128]{1,0:T(8,128)(2,1)}, bf16[1024,128]{1,0:T(8,128)(2,1)S(1)}, u32[]{:S(2)}, u32[]{:S(2)}) collective-permute-start(bf16[1024,128]{1,0:T(8,128)(2,1)} %first_ref.1), channel_id=1, source_target_pairs={{0,64},{64,0},{128,192},{192,128},{1,65},{65,1},{129,193},{193,129... | collective-permute-start | bytes 786440 | tf_op jit(solution)/shard_map/ppermute | solution.py:124
  10.6 12.7 %collective-permute-start.5 = (bf16[1024,128]{1,0:T(8,128)(2,1)}, bf16[1024,128]{1,0:T(8,128)(2,1)S(1)}, u32[]{:S(2)}, u32[]{:S(2)}) collective-permute-start(bf16[1024,128]{1,0:T(8,128)(2,1)} %first_ref.1), channel_id=1, source_target_pairs={{0,256},{256,0},{1,257},{257,1},{2,258},{258,2},{3,259},{259,3},{4... | collective-permute-start | bytes 786440 | tf_op jit(solution)/shard_map/ppermute | solution.py:127
  17.6 1.0 %copy-start.1 = (bf16[1024,128]{1,0:T(8,128)(2,1)S(1)}, bf16[1024,128]{1,0:T(8,128)(2,1)}, u32[]{:S(2)}) copy-start(bf16[1024,128]{1,0:T(8,128)(2,1)} %first_ref.1) | copy-start | bytes 786436
  18.7 4.6 %copy-start.2 = (bf16[1024,128]{1,0:T(8,128)(2,1)S(1)}, bf16[1024,128]{1,0:T(8,128)(2,1)}, u32[]{:S(2)}) copy-start(bf16[1024,128]{1,0:T(8,128)(2,1)} %first_ref.1) | copy-start | bytes 786436
  18.7 4.6 %copy-start.4 = (f32[1024]{0:T(1024)S(1)}, f32[1024]{0:T(1024)}, u32[]{:S(2)}) copy-start(f32[1024]{0:T(1024)} %param.5) | copy-start | bytes 12292
  18.7 4.8 %collective-permute-start.4 = (bf16[2,1024,128]{2,1,0:T(8,128)(2,1)S(1)}, bf16[2,1024,128]{2,1,0:T(8,128)(2,1)S(1)}, u32[]{:S(2)}, u32[]{:S(2)}) collective-permute-start(bf16[2,1024,128]{2,1,0:T(8,128)(2,1)S(1)} %stack_one.1.refs_0_.one_ref), channel_id=1, source_target_pairs={{0,32},{32,0},{1,33},{33,1},{2,34},{34,2},{3,35},{35,3},{4,36},{36... | collective-permute-start | bytes 1572872 | tf_op jit(solution)/shard_map/ppermute | solution.py:130
  20.8 3.9 %collective-permute-start.2 = (bf16[2,1024,128]{2,1,0:T(8,128)(2,1)S(1)}, bf16[2,1024,128]{2,1,0:T(8,128)(2,1)S(1)}, u32[]{:S(2)}, u32[]{:S(2)}) collective-permute-start(bf16[2,1024,128]{2,1,0:T(8,128)(2,1)S(1)} %stack_two.1.refs_1_.two_ref), channel_id=1, source_target_pairs={{0,32},{32,0},{1,33},{33,1},{2,34},{34,2},{3,35},{35,3},{4,36},{36... | collective-permute-start | bytes 1572872 | tf_op jit(solution)/shard_map/ppermute | solution.py:132
  25.1 32.2 %copy-start = (bf16[2048,256]{1,0:T(8,128)(2,1)S(1)}, bf16[2048,256]{1,0:T(8,128)(2,1)}, u32[]{:S(2)}) copy-start(bf16[2048,256]{1,0:T(8,128)(2,1)} %eigvec_ref) | copy-start | bytes 3145732
  47.7 9.5 %copy-start.3 = (s32[2048]{0:T(1024)S(1)}, s32[2048]{0:T(1024)}, u32[]{:S(2)}) copy-start(s32[2048]{0:T(1024)} %param.7) | copy-start | bytes 24580
  47.7 18.6 %all-to-all-start.1 = ((f32[4,64,128]{2,1,0:T(8,128)}), f32[4,64,128]{2,1,0:T(8,128)S(1)}, u32[]{:S(2)}, u32[]{:S(2)}) async-start(f32[4,64,128]{2,1,0:T(8,128)} %sum_y.1), calls=%async_computation.1 | async-start | bytes 262144 | tf_op jit(solution)/shard_map/all_to_all | solution.py:155
  59.5 6.2 %collective-permute-start.6 = (f32[16,1024]{1,0:T(8,128)S(1)}, f32[16,1024]{1,0:T(8,128)S(1)}, u32[]{:S(2)}, u32[]{:S(2)}) collective-permute-start(f32[16,1024]{1,0:T(8,128)S(1)} %get-tuple-element.23), channel_id=1, source_target_pairs={{0,256},{256,0},{1,257},{257,1},{2,258},{258,2},{3,259},{259,3},{4... | collective-permute-start | bytes 196616 | tf_op jit(solution)/shard_map/ppermute | solution.py:162

commit v7 on v6

--- a/solution.py
+++ b/solution.py
@@ -6,6 +6,7 @@
 from jax.sharding import Mesh, PartitionSpec as P
 
 SWAP = [(0, 1), (1, 0)]
+SPACE = ("z2", "z1", "zl", "yh1", "yh0")
 HIDE = 20 * 10**9
 VMEM = pl.BlockSpec(memory_space=pltpu.VMEM)
 
@@ -77,7 +78,7 @@
 
     def store(k, corner, tile):
         y2, core1, x1 = (y, 1 - y)[corner // 2], (core, 1 - core)[k // 4], places[k % 4]
-        out_ref[(core1 * 2 + corner % 2) * 4 + x1 % 2 * 2 + y2, x1 // 2] = tile
+        out_ref[x1 % 2 * 8 + corner % 2 * 4 + core1 * 2 + y2, x1 // 2] = tile
 
     for k in range(6):
         for corner in range(4):
@@ -104,7 +105,7 @@
             total = parts_ref[y1, high].astype(jnp.float32)
             for k in range(1, 8):
                 total += parts_ref[k * 2 + y1, high].astype(jnp.float32)
-            out_ref[y1 * 2 + high] = total * scaling
+            out_ref[high * 2 + y1] = total * scaling
 
 
 def last_kernel(parts_ref, stay_ref, away_ref, gram_ref, modes_ref):
@@ -117,7 +118,7 @@
 
 def body(snapshots, cell_weight, eigvec, time_index):
     rows, width = snapshots.shape
-    scaling = 1.0 / (rows * lax.axis_size("zh") * lax.axis_size("zl") * lax.axis_size("yh"))
+    scaling = 1.0 / (rows * lax.axis_size(SPACE))
     shape = jax.ShapeDtypeStruct
 
     def trade(k):
@@ -147,12 +148,12 @@
     parts = local(
         gram_end_kernel, shape((16, 2, 64, 128), jnp.bfloat16), two_other, weighted, begun, name="gram_end"
     )
-    parts = lax.all_to_all(parts, ("yh", "zl", "yl"), 0, 0, tiled=True)
+    parts = lax.all_to_all(parts, ("zl", "yh0", "yh1", "yl"), 0, 0, tiled=True)
     parts = local(lambda *refs: sum_kernel(scaling, *refs), shape((4, 64, 128), jnp.float32), parts, name="sum_y")
     parts, one, two, one_other, two_other, time_index, eigvec = lax.optimization_barrier(
         (parts, one, two, one_other, two_other, time_index, eigvec)
     )
-    parts = lax.all_to_all(parts, "zh", 0, 0, tiled=True)
+    parts = lax.all_to_all(parts, ("z1", "z2"), 0, 0, tiled=True)
     ordered = local(
         ordered_kernel, shape((2, 4, 32, 128), jnp.bfloat16), time_index.reshape(16, 128), eigvec, name="ordered"
     )
@@ -166,8 +167,8 @@
 
 
 def solution(mesh):
-    fine = Mesh(mesh.devices.reshape(2, 4, 2, 4, 2, 4), ("yl", "x", "core", "zh", "zl", "yh"))
-    snap, space = ("yl", "x", "core"), ("zh", "zl", "yh")
+    fine = Mesh(mesh.devices.reshape(2, 4, 2, 2, 2, 2, 2, 2), ("yl", "x", "core") + SPACE)
+    snap, space = ("yl", "x", "core"), SPACE
     in_specs = (P(space, snap), P(space), P(), P())
     out_specs = (P(space, snap), P(snap, space))
     return jax.shard_map(body, mesh=fine, in_specs=in_specs, out_specs=out_specs, check_vma=False)

time: 67.5 us -> 66.9 us (level)
  starting transfers between devices: 33.9 us -> 33.1 us
    ppermute x1, starting transfers between devices: 2.95 us -> 2.11 us  [body(): away = lax.ppermute(away, 'yl', SWAP)]
    ppermute x1, waiting for transfers between devices: 3.22 us -> 4.06 us  [body(): away = lax.ppermute(away, 'yl', SWAP)]
  transfers between devices with their start and end apart: 8 -> 8, of which waited for: 3 -> 2; matrix products, arithmetic and copies ran while one was open for 0% -> 0% of each run, Pallas kernels for 4% -> 4%
where the time goes in v7:
time: 66.9 us; the launch traced here: 66.4 us
  starting transfers between devices  33.1 us (49%)
  blocking collectives  21.9 us (33%)
  waiting for transfers between devices  4.71 us (7%)
  Pallas kernels  4.7 us (7%)
  local copies, waits for them, and re-layouts  1 us (1%)
  between operations  0.82 us (1%)
    all_to_all x1, blocking collectives, body(): parts = lax.all_to_all(parts, ('zl', 'yh0', 'yh1', 'yl'), 0, 0, tiled=True)  21.9 us
    ppermute x3, starting transfers between devices, trade(): return lax.ppermute(snapshots, 'x', [(i, i ^ k) for i in range(4)])  9.91 us
    all_to_all x1, starting transfers between devices, body(): parts = lax.all_to_all(parts, ('z1', 'z2'), 0, 0, tiled=True)  9.53 us
    ppermute x1, starting transfers between devices, body(): partner = lax.ppermute(snapshots, 'yl', SWAP)  7.05 us
    pallas_call x8, Pallas kernels, local(): pl.pallas_call(kernel, out_shape=out_shape, in_specs=[VMEM] * len(operand...  4.7 us
    ppermute x1, waiting for transfers between devices, body(): away = lax.ppermute(away, 'yl', SWAP)  4.06 us
    ppermute x1, starting transfers between devices, body(): two_other = lax.ppermute(two, 'core', SWAP)  2.41 us
    ppermute x1, starting transfers between devices, body(): away = lax.ppermute(away, 'yl', SWAP)  2.11 us
  transfers between devices with their start and end apart: 8, of which 2 were waited for; matrix products, arithmetic and copies ran while one was open for 0% of the time, Pallas kernels for 4%

profile of v7, /device:TPU:8, one launch (start us, length us, event | category | flops | bytes accessed | tf_op | source)
XLA Modules:
  0.0 66.4 jit_solution(7974043622846048424)
XLA Ops:
  0.6 4.9 %collective-permute-start.3 = (bf16[1024,128]{1,0:T(8,128)(2,1)}, bf16[1024,128]{1,0:T(8,128)(2,1)S(1)}, u32[]{:S(2)}, u32[]{:S(2)}) collective-permute-start(bf16[1024,128]{1,0:T(8,128)(2,1)} %first_ref.1), channel_id=1, source_target_pairs={{0,128},{64,192},{128,0},{192,64},{1,129},{65,193},{129,1},{193,65... | collective-permute-start | bytes 786440 | tf_op jit(solution)/shard_map/ppermute | solution.py:125
  5.6 3.1 %collective-permute-start.1 = (bf16[1024,128]{1,0:T(8,128)(2,1)}, bf16[1024,128]{1,0:T(8,128)(2,1)S(1)}, u32[]{:S(2)}, u32[]{:S(2)}) collective-permute-start(bf16[1024,128]{1,0:T(8,128)(2,1)} %first_ref.1), channel_id=1, source_target_pairs={{0,192},{64,128},{128,64},{192,0},{1,193},{65,129},{129,65},{193,1... | collective-permute-start | bytes 786440 | tf_op jit(solution)/shard_map/ppermute | solution.py:125
  8.6 1.9 %collective-permute-start = (bf16[1024,128]{1,0:T(8,128)(2,1)}, bf16[1024,128]{1,0:T(8,128)(2,1)S(1)}, u32[]{:S(2)}, u32[]{:S(2)}) collective-permute-start(bf16[1024,128]{1,0:T(8,128)(2,1)} %first_ref.1), channel_id=1, source_target_pairs={{0,64},{64,0},{128,192},{192,128},{1,65},{65,1},{129,193},{193,129... | collective-permute-start | bytes 786440 | tf_op jit(solution)/shard_map/ppermute | solution.py:125
  10.6 7.0 %collective-permute-start.5 = (bf16[1024,128]{1,0:T(8,128)(2,1)}, bf16[1024,128]{1,0:T(8,128)(2,1)S(1)}, u32[]{:S(2)}, u32[]{:S(2)}) collective-permute-start(bf16[1024,128]{1,0:T(8,128)(2,1)} %first_ref.1), channel_id=1, source_target_pairs={{0,256},{256,0},{1,257},{257,1},{2,258},{258,2},{3,259},{259,3},{4... | collective-permute-start | bytes 786440 | tf_op jit(solution)/shard_map/ppermute | solution.py:128
  17.6 0.0 collective-permute-done.3.second_ref
  17.6 0.0 copy-start.1
  17.6 1.0 %copy-done.1 = bf16[1024,128]{1,0:T(8,128)(2,1)S(1)} copy-done((bf16[1024,128]{1,0:T(8,128)(2,1)S(1)}, bf16[1024,128]{1,0:T(8,128)(2,1)}, u32[]{:S(2)}) %copy-start.1) | copy-done | bytes 262168
  18.7 0.0 copy-start.2
  18.7 0.0 copy-start.4
  18.7 2.1 %collective-permute-start.4 = (bf16[2,1024,128]{2,1,0:T(8,128)(2,1)S(1)}, bf16[2,1024,128]{2,1,0:T(8,128)(2,1)S(1)}, u32[]{:S(2)}, u32[]{:S(2)}) collective-permute-start(bf16[2,1024,128]{2,1,0:T(8,128)(2,1)S(1)} %stack_one.1.refs_0_.one_ref), channel_id=1, source_target_pairs={{0,32},{32,0},{1,33},{33,1},{2,34},{34,2},{3,35},{35,3},{4,36},{36... | collective-permute-start | bytes 1572872 | tf_op jit(solution)/shard_map/ppermute | solution.py:131
  20.7 0.0 collective-permute-done.1.second_ref
  20.7 0.0 collective-permute-done.first_ref
  20.8 2.4 %collective-permute-start.2 = (bf16[2,1024,128]{2,1,0:T(8,128)(2,1)S(1)}, bf16[2,1024,128]{2,1,0:T(8,128)(2,1)S(1)}, u32[]{:S(2)}, u32[]{:S(2)}) collective-permute-start(bf16[2,1024,128]{2,1,0:T(8,128)(2,1)S(1)} %stack_two.1.refs_1_.two_ref), channel_id=1, source_target_pairs={{0,32},{32,0},{1,33},{33,1},{2,34},{34,2},{3,35},{35,3},{4,36},{36... | collective-permute-start | bytes 1572872 | tf_op jit(solution)/shard_map/ppermute | solution.py:133
  23.2 0.0 collective-permute-done.5
  23.2 0.0 copy-done.2
  23.2 0.0 copy-done.4
  23.2 0.2 multiply_convert_fusion.refs_3_.weighted_ref
  23.5 0.0 collective-permute-done.4.refs_2_.one_other_ref
  23.5 0.6 gram_begin.1.begun_ref
  24.1 0.6 collective-permute-done.2.last_ref.two_other_ref
  24.7 0.3 gram_end.1
  25.1 0.0 copy-start
  25.1 21.9 %all_to_all.10.refs_0_ = bf16[16,2,64,128]{3,2,1,0:T(8,128)(2,1)S(1)} all-to-all(bf16[16,2,64,128]{3,2,1,0:T(8,128)(2,1)S(1)} %gram_end.1), channel_id=1, replica_groups=mesh['yl'=2,'x'=4,'core'=2,'z2'=2,'z1'=2,'zl'=2,'yh1'=2,'yh0'=2] {'zl','..., dimensions={0} | all-to-all | bytes 1048576 | tf_op jit(solution)/shard_map/all_to_all | solution.py:151
  47.0 0.7 %sum_y.1 = f32[4,64,128]{2,1,0:T(8,128)} custom-call(bf16[16,2,64,128]{3,2,1,0:T(8,128)(2,1)S(1)} %all_to_all.10.refs_0_), custom_call_target="tpu_custom_call" | custom-call | tf_op jit(solution)/shard_map/sum_y/pallas_call | solution.py:16
  47.8 0.0 copy-start.3
  47.8 9.5 %all-to-all-start.1 = ((f32[4,64,128]{2,1,0:T(8,128)}), f32[4,64,128]{2,1,0:T(8,128)S(1)}, u32[]{:S(2)}, u32[]{:S(2)}) async-start(f32[4,64,128]{2,1,0:T(8,128)} %sum_y.1), calls=%async_computation.1 | async-start | bytes 262144 | tf_op jit(solution)/shard_map/all_to_all | solution.py:156
  57.3 0.0 copy-done
  57.3 0.0 copy-done.3
  57.3 1.5 %ordered.1.ordered_ref = bf16[2,4,32,128]{3,2,1,0:T(8,128)(2,1)S(1)} custom-call(s32[16,128]{1,0:T(8,128)S(1)} %bitcast.1, bf16[2048,256]{1,0:T(8,128)(2,1)S(1)} %copy-done), custom_call_target="tpu_custom_call" | custom-call | tf_op jit(solution)/shard_map/ordered/pallas_call | solution.py:16
  58.8 0.8 %mode_parts.1 = (f32[16,1024]{1,0:T(8,128)S(1)}, f32[16,1024]{1,0:T(8,128)S(1)}) custom-call(bf16[2,1024,128]{2,1,0:T(8,128)(2,1)S(1)} %stack_one.1.refs_0_.one_ref, bf16[2,1024,128]{2,1,0:T(8,128)(2,1)S(1)} %stack_two.1.refs_1_.two_ref, bf16[2,1024,128]{2,1,0:T(8,128)(2,1)S(1)} %collective-permute-done.4.refs_2_.one_other_ref, ...), custom_call_target="tpu_custom_call" | custom-call | tf_op jit(solution)/shard_map/mode_parts/pallas_call | solution.py:16
  59.6 2.1 %collective-permute-start.6 = (f32[16,1024]{1,0:T(8,128)S(1)}, f32[16,1024]{1,0:T(8,128)S(1)}, u32[]{:S(2)}, u32[]{:S(2)}) collective-permute-start(f32[16,1024]{1,0:T(8,128)S(1)} %get-tuple-element.23), channel_id=1, source_target_pairs={{0,256},{256,0},{1,257},{257,1},{2,258},{258,2},{3,259},{259,3},{4... | collective-permute-start | bytes 196616 | tf_op jit(solution)/shard_map/ppermute | solution.py:163
  61.7 4.1 %collective-permute-done.6.away_ref = f32[16,1024]{1,0:T(8,128)S(1)} collective-permute-done((f32[16,1024]{1,0:T(8,128)S(1)}, f32[16,1024]{1,0:T(8,128)S(1)}, u32[]{:S(2)}, u32[]{:S(2)}) %collective-permute-start.6) | collective-permute-done | bytes 65568 | tf_op jit(solution)/shard_map/ppermute | solution.py:163
  65.8 0.0 all-to-all-done.1.parts_ref
  65.8 0.7 sum_z.1
  (2 shorter events, 0.1 us)
Async XLA Ops:
  0.6 17.0 %collective-permute-start.3 = (bf16[1024,128]{1,0:T(8,128)(2,1)}, bf16[1024,128]{1,0:T(8,128)(2,1)S(1)}, u32[]{:S(2)}, u32[]{:S(2)}) collective-permute-start(bf16[1024,128]{1,0:T(8,128)(2,1)} %first_ref.1), channel_id=1, source_target_pairs={{0,128},{64,192},{128,0},{192,64},{1,129},{65,193},{129,1},{193,65... | collective-permute-start | bytes 786440 | tf_op jit(solution)/shard_map/ppermute | solution.py:125
  5.6 15.2 %collective-permute-start.1 = (bf16[1024,128]{1,0:T(8,128)(2,1)}, bf16[1024,128]{1,0:T(8,128)(2,1)S(1)}, u32[]{:S(2)}, u32[]{:S(2)}) collective-permute-start(bf16[1024,128]{1,0:T(8,128)(2,1)} %first_ref.1), channel_id=1, source_target_pairs={{0,192},{64,128},{128,64},{192,0},{1,193},{65,129},{129,65},{193,1... | collective-permute-start | bytes 786440 | tf_op jit(solution)/shard_map/ppermute | solution.py:125
  8.6 12.1 %collective-permute-start = (bf16[1024,128]{1,0:T(8,128)(2,1)}, bf16[1024,128]{1,0:T(8,128)(2,1)S(1)}, u32[]{:S(2)}, u32[]{:S(2)}) collective-permute-start(bf16[1024,128]{1,0:T(8,128)(2,1)} %first_ref.1), channel_id=1, source_target_pairs={{0,64},{64,0},{128,192},{192,128},{1,65},{65,1},{129,193},{193,129... | collective-permute-start | bytes 786440 | tf_op jit(solution)/shard_map/ppermute | solution.py:125
  10.6 12.7 %collective-permute-start.5 = (bf16[1024,128]{1,0:T(8,128)(2,1)}, bf16[1024,128]{1,0:T(8,128)(2,1)S(1)}, u32[]{:S(2)}, u32[]{:S(2)}) collective-permute-start(bf16[1024,128]{1,0:T(8,128)(2,1)} %first_ref.1), channel_id=1, source_target_pairs={{0,256},{256,0},{1,257},{257,1},{2,258},{258,2},{3,259},{259,3},{4... | collective-permute-start | bytes 786440 | tf_op jit(solution)/shard_map/ppermute | solution.py:128
  17.6 1.0 %copy-start.1 = (bf16[1024,128]{1,0:T(8,128)(2,1)S(1)}, bf16[1024,128]{1,0:T(8,128)(2,1)}, u32[]{:S(2)}) copy-start(bf16[1024,128]{1,0:T(8,128)(2,1)} %first_ref.1) | copy-start | bytes 786436
  18.7 4.6 %copy-start.2 = (bf16[1024,128]{1,0:T(8,128)(2,1)S(1)}, bf16[1024,128]{1,0:T(8,128)(2,1)}, u32[]{:S(2)}) copy-start(bf16[1024,128]{1,0:T(8,128)(2,1)} %first_ref.1) | copy-start | bytes 786436
  18.7 4.6 %copy-start.4 = (f32[1024]{0:T(1024)S(1)}, f32[1024]{0:T(1024)}, u32[]{:S(2)}) copy-start(f32[1024]{0:T(1024)} %param.5) | copy-start | bytes 12292
  18.7 4.8 %collective-permute-start.4 = (bf16[2,1024,128]{2,1,0:T(8,128)(2,1)S(1)}, bf16[2,1024,128]{2,1,0:T(8,128)(2,1)S(1)}, u32[]{:S(2)}, u32[]{:S(2)}) collective-permute-start(bf16[2,1024,128]{2,1,0:T(8,128)(2,1)S(1)} %stack_one.1.refs_0_.one_ref), channel_id=1, source_target_pairs={{0,32},{32,0},{1,33},{33,1},{2,34},{34,2},{3,35},{35,3},{4,36},{36... | collective-permute-start | bytes 1572872 | tf_op jit(solution)/shard_map/ppermute | solution.py:131
  20.8 3.9 %collective-permute-start.2 = (bf16[2,1024,128]{2,1,0:T(8,128)(2,1)S(1)}, bf16[2,1024,128]{2,1,0:T(8,128)(2,1)S(1)}, u32[]{:S(2)}, u32[]{:S(2)}) collective-permute-start(bf16[2,1024,128]{2,1,0:T(8,128)(2,1)S(1)} %stack_two.1.refs_1_.two_ref), channel_id=1, source_target_pairs={{0,32},{32,0},{1,33},{33,1},{2,34},{34,2},{3,35},{35,3},{4,36},{36... | collective-permute-start | bytes 1572872 | tf_op jit(solution)/shard_map/ppermute | solution.py:133
  25.1 32.2 %copy-start = (bf16[2048,256]{1,0:T(8,128)(2,1)S(1)}, bf16[2048,256]{1,0:T(8,128)(2,1)}, u32[]{:S(2)}) copy-start(bf16[2048,256]{1,0:T(8,128)(2,1)} %eigvec_ref) | copy-start | bytes 3145732
  47.8 9.5 %copy-start.3 = (s32[2048]{0:T(1024)S(1)}, s32[2048]{0:T(1024)}, u32[]{:S(2)}) copy-start(s32[2048]{0:T(1024)} %param.7) | copy-start | bytes 24580
  47.8 18.0 %all-to-all-start.1 = ((f32[4,64,128]{2,1,0:T(8,128)}), f32[4,64,128]{2,1,0:T(8,128)S(1)}, u32[]{:S(2)}, u32[]{:S(2)}) async-start(f32[4,64,128]{2,1,0:T(8,128)} %sum_y.1), calls=%async_computation.1 | async-start | bytes 262144 | tf_op jit(solution)/shard_map/all_to_all | solution.py:156
  59.6 6.2 %collective-permute-start.6 = (f32[16,1024]{1,0:T(8,128)S(1)}, f32[16,1024]{1,0:T(8,128)S(1)}, u32[]{:S(2)}, u32[]{:S(2)}) collective-permute-start(f32[16,1024]{1,0:T(8,128)S(1)} %get-tuple-element.23), channel_id=1, source_target_pairs={{0,256},{256,0},{1,257},{257,1},{2,258},{258,2},{3,259},{259,3},{4... | collective-permute-start | bytes 196616 | tf_op jit(solution)/shard_map/ppermute | solution.py:163

commit v8 on v7

--- a/solution.py
+++ b/solution.py
@@ -86,17 +86,19 @@
     gram_blocks(last_ref, weighted_ref, lambda k, corner, tile: store(6 + k, corner, tile))
 
 
-def modes_kernel(one_ref, two_ref, one_other_ref, two_other_ref, ordered_ref, away_ref, stay_ref):
-    core, places = lax.axis_index("core"), shifts()
-    total = jnp.zeros((32, stay_ref.shape[1]), jnp.float32)
+def modes_kernel(keeper, one_ref, two_ref, one_other_ref, two_other_ref, ordered_ref, out_ref):
+    y, core, places = lax.axis_index("yl"), lax.axis_index("core"), shifts()
+    kept = pl.ds(((y + keeper) % 2) * 16, 16)
+    total = jnp.zeros(out_ref.shape, jnp.float32)
     for refs, core1 in (((one_ref, two_ref), core), ((one_other_ref, two_other_ref), 1 - core)):
         for k, x1 in enumerate(places):
             total += lax.dot_general(
-                ordered_ref[core1, x1], refs[k // 2][k % 2], (((1,), (1,)), ((), ())), preferred_element_type=jnp.float32
+                ordered_ref[core1, x1, kept],
+                refs[k // 2][k % 2],
+                (((1,), (1,)), ((), ())),
+                preferred_element_type=jnp.float32,
             )
-    first = lax.axis_index("yl") == 0
-    stay_ref[...] = jnp.where(first, total[:16], total[16:])
-    away_ref[...] = jnp.where(first, total[16:], total[:16])
+    out_ref[...] = total
 
 
 def sum_kernel(scaling, parts_ref, out_ref):
@@ -159,8 +161,10 @@
     )
     half = shape((16, rows), jnp.float32)
     blocks = one, two, one_other, two_other
-    away, stay = local(modes_kernel, [half, half], *blocks, ordered, name="mode_parts")
+    away = local(lambda *refs: modes_kernel(1, *refs), half, *blocks, ordered, name="modes_away")
+    away, ordered = lax.optimization_barrier((away, ordered))
     away = lax.ppermute(away, "yl", SWAP)
+    stay = local(lambda *refs: modes_kernel(0, *refs), half, *blocks, ordered, name="modes_stay")
     outs = [shape((64, 128), jnp.float32), half]
     gram, modes = local(last_kernel, outs, parts, stay, away, name="sum_z")
     return gram, modes

time: 66.9 us -> 66.8 us (level)
    pallas_call x8 -> x9, Pallas kernels: 4.7 us -> 5.22 us  [local(): pl.pallas_call(kernel, out_shape=out_shape, in_specs=[VMEM] * len(operand...]
  transfers between devices with their start and end apart: 8 -> 8, of which waited for: 2 -> 2; matrix products, arithmetic and copies ran while one was open for 0% -> 0% of each run, Pallas kernels for 4% -> 5%
where the time goes in v8:
time: 66.8 us; the launch traced here: 66.3 us
  starting transfers between devices  33 us (49%)
  blocking collectives  21.9 us (33%)
  Pallas kernels  5.22 us (8%)
  waiting for transfers between devices  4.1 us (6%)
  local copies, waits for them, and re-layouts  1 us (1%)
  between operations  0.81 us (1%)
    all_to_all x1, blocking collectives, body(): parts = lax.all_to_all(parts, ('zl', 'yh0', 'yh1', 'yl'), 0, 0, tiled=True)  21.9 us
    ppermute x3, starting transfers between devices, trade(): return lax.ppermute(snapshots, 'x', [(i, i ^ k) for i in range(4)])  9.91 us
    all_to_all x1, starting transfers between devices, body(): parts = lax.all_to_all(parts, ('z1', 'z2'), 0, 0, tiled=True)  9.53 us
    ppermute x1, starting transfers between devices, body(): partner = lax.ppermute(snapshots, 'yl', SWAP)  7.05 us
    pallas_call x9, Pallas kernels, local(): pl.pallas_call(kernel, out_shape=out_shape, in_specs=[VMEM] * len(operand...  5.22 us
    ppermute x1, waiting for transfers between devices, body(): away = lax.ppermute(away, 'yl', SWAP)  3.43 us
    ppermute x1, starting transfers between devices, body(): two_other = lax.ppermute(two, 'core', SWAP)  2.41 us
    ppermute x1, starting transfers between devices, body(): away = lax.ppermute(away, 'yl', SWAP)  2.1 us
  transfers between devices with their start and end apart: 8, of which 2 were waited for; matrix products, arithmetic and copies ran while one was open for 0% of the time, Pallas kernels for 5%

profile of v8, /device:TPU:8, one launch (start us, length us, event | category | flops | bytes accessed | tf_op | source)
XLA Modules:
  0.0 66.3 jit_solution(17774591769498065273)
XLA Ops:
  0.6 4.9 %collective-permute-start.3 = (bf16[1024,128]{1,0:T(8,128)(2,1)}, bf16[1024,128]{1,0:T(8,128)(2,1)S(1)}, u32[]{:S(2)}, u32[]{:S(2)}) collective-permute-start(bf16[1024,128]{1,0:T(8,128)(2,1)} %first_ref.1), channel_id=1, source_target_pairs={{0,128},{64,192},{128,0},{192,64},{1,129},{65,193},{129,1},{193,65... | collective-permute-start | bytes 786440 | tf_op jit(solution)/shard_map/ppermute | solution.py:127
  5.6 3.1 %collective-permute-start.1 = (bf16[1024,128]{1,0:T(8,128)(2,1)}, bf16[1024,128]{1,0:T(8,128)(2,1)S(1)}, u32[]{:S(2)}, u32[]{:S(2)}) collective-permute-start(bf16[1024,128]{1,0:T(8,128)(2,1)} %first_ref.1), channel_id=1, source_target_pairs={{0,192},{64,128},{128,64},{192,0},{1,193},{65,129},{129,65},{193,1... | collective-permute-start | bytes 786440 | tf_op jit(solution)/shard_map/ppermute | solution.py:127
  8.6 1.9 %collective-permute-start = (bf16[1024,128]{1,0:T(8,128)(2,1)}, bf16[1024,128]{1,0:T(8,128)(2,1)S(1)}, u32[]{:S(2)}, u32[]{:S(2)}) collective-permute-start(bf16[1024,128]{1,0:T(8,128)(2,1)} %first_ref.1), channel_id=1, source_target_pairs={{0,64},{64,0},{128,192},{192,128},{1,65},{65,1},{129,193},{193,129... | collective-permute-start | bytes 786440 | tf_op jit(solution)/shard_map/ppermute | solution.py:127
  10.6 7.0 %collective-permute-start.5 = (bf16[1024,128]{1,0:T(8,128)(2,1)}, bf16[1024,128]{1,0:T(8,128)(2,1)S(1)}, u32[]{:S(2)}, u32[]{:S(2)}) collective-permute-start(bf16[1024,128]{1,0:T(8,128)(2,1)} %first_ref.1), channel_id=1, source_target_pairs={{0,256},{256,0},{1,257},{257,1},{2,258},{258,2},{3,259},{259,3},{4... | collective-permute-start | bytes 786440 | tf_op jit(solution)/shard_map/ppermute | solution.py:130
  17.6 0.0 collective-permute-done.3.second_ref
  17.6 0.0 copy-start.1
  17.6 1.0 %copy-done.1 = bf16[1024,128]{1,0:T(8,128)(2,1)S(1)} copy-done((bf16[1024,128]{1,0:T(8,128)(2,1)S(1)}, bf16[1024,128]{1,0:T(8,128)(2,1)}, u32[]{:S(2)}) %copy-start.1) | copy-done | bytes 262168
  18.7 0.0 copy-start.2
  18.7 0.0 copy-start.4
  18.7 2.1 %collective-permute-start.4 = (bf16[2,1024,128]{2,1,0:T(8,128)(2,1)S(1)}, bf16[2,1024,128]{2,1,0:T(8,128)(2,1)S(1)}, u32[]{:S(2)}, u32[]{:S(2)}) collective-permute-start(bf16[2,1024,128]{2,1,0:T(8,128)(2,1)S(1)} %stack_one.1.refs_0_), channel_id=1, source_target_pairs={{0,32},{32,0},{1,33},{33,1},{2,34},{34,2},{3,35},{35,3},{4,36},{36... | collective-permute-start | bytes 1572872 | tf_op jit(solution)/shard_map/ppermute | solution.py:133
  20.7 0.0 collective-permute-done.1.second_ref
  20.7 0.0 collective-permute-done.first_ref
  20.8 2.4 %collective-permute-start.2 = (bf16[2,1024,128]{2,1,0:T(8,128)(2,1)S(1)}, bf16[2,1024,128]{2,1,0:T(8,128)(2,1)S(1)}, u32[]{:S(2)}, u32[]{:S(2)}) collective-permute-start(bf16[2,1024,128]{2,1,0:T(8,128)(2,1)S(1)} %stack_two.1.refs_1_), channel_id=1, source_target_pairs={{0,32},{32,0},{1,33},{33,1},{2,34},{34,2},{3,35},{35,3},{4,36},{36... | collective-permute-start | bytes 1572872 | tf_op jit(solution)/shard_map/ppermute | solution.py:135
  23.2 0.0 collective-permute-done.5
  23.2 0.0 copy-done.2
  23.2 0.0 copy-done.4
  23.2 0.2 multiply_convert_fusion.refs_3_.weighted_ref
  23.5 0.0 collective-permute-done.4.refs_2_
  23.5 0.6 gram_begin.1.begun_ref
  24.1 0.6 collective-permute-done.2.last_ref.refs_3_
  24.7 0.3 gram_end.1
  25.1 0.0 copy-start
  25.1 21.9 %all_to_all.10.refs_0_ = bf16[16,2,64,128]{3,2,1,0:T(8,128)(2,1)S(1)} all-to-all(bf16[16,2,64,128]{3,2,1,0:T(8,128)(2,1)S(1)} %gram_end.1), channel_id=1, replica_groups=mesh['yl'=2,'x'=4,'core'=2,'z2'=2,'z1'=2,'zl'=2,'yh1'=2,'yh0'=2] {'zl','..., dimensions={0} | all-to-all | bytes 1048576 | tf_op jit(solution)/shard_map/all_to_all | solution.py:153
  47.0 0.7 %sum_y.1 = f32[4,64,128]{2,1,0:T(8,128)} custom-call(bf16[16,2,64,128]{3,2,1,0:T(8,128)(2,1)S(1)} %all_to_all.10.refs_0_), custom_call_target="tpu_custom_call" | custom-call | tf_op jit(solution)/shard_map/sum_y/pallas_call | solution.py:16
  47.8 0.0 copy-start.3
  47.8 9.5 %all-to-all-start.1 = ((f32[4,64,128]{2,1,0:T(8,128)}), f32[4,64,128]{2,1,0:T(8,128)S(1)}, u32[]{:S(2)}, u32[]{:S(2)}) async-start(f32[4,64,128]{2,1,0:T(8,128)} %sum_y.1), calls=%async_computation.1 | async-start | bytes 262144 | tf_op jit(solution)/shard_map/all_to_all | solution.py:158
  57.3 0.0 copy-done
  57.3 0.0 copy-done.3
  57.3 1.5 %ordered.1.refs_4_ = bf16[2,4,32,128]{3,2,1,0:T(8,128)(2,1)S(1)} custom-call(s32[16,128]{1,0:T(8,128)S(1)} %bitcast.1, bf16[2048,256]{1,0:T(8,128)(2,1)S(1)} %copy-done), custom_call_target="tpu_custom_call" | custom-call | tf_op jit(solution)/shard_map/ordered/pallas_call | solution.py:16
  58.8 0.6 modes_away.1
  59.5 2.1 %collective-permute-start.6 = (f32[16,1024]{1,0:T(8,128)S(1)}, f32[16,1024]{1,0:T(8,128)S(1)}, u32[]{:S(2)}, u32[]{:S(2)}) collective-permute-start(f32[16,1024]{1,0:T(8,128)S(1)} %modes_away.1), channel_id=1, source_target_pairs={{0,256},{256,0},{1,257},{257,1},{2,258},{258,2},{3,259},{259,3},{4... | collective-permute-start | bytes 196616 | tf_op jit(solution)/shard_map/ppermute | solution.py:166
  61.6 0.6 modes_stay.1.stay_ref
  62.2 3.4 %collective-permute-done.6.away_ref = f32[16,1024]{1,0:T(8,128)S(1)} collective-permute-done((f32[16,1024]{1,0:T(8,128)S(1)}, f32[16,1024]{1,0:T(8,128)S(1)}, u32[]{:S(2)}, u32[]{:S(2)}) %collective-permute-start.6) | collective-permute-done | bytes 65568 | tf_op jit(solution)/shard_map/ppermute | solution.py:166
  65.6 0.0 all-to-all-done.1.parts_ref
  65.7 0.7 sum_z.1
  (2 shorter events, 0.1 us)
Async XLA Ops:
  0.6 17.0 %collective-permute-start.3 = (bf16[1024,128]{1,0:T(8,128)(2,1)}, bf16[1024,128]{1,0:T(8,128)(2,1)S(1)}, u32[]{:S(2)}, u32[]{:S(2)}) collective-permute-start(bf16[1024,128]{1,0:T(8,128)(2,1)} %first_ref.1), channel_id=1, source_target_pairs={{0,128},{64,192},{128,0},{192,64},{1,129},{65,193},{129,1},{193,65... | collective-permute-start | bytes 786440 | tf_op jit(solution)/shard_map/ppermute | solution.py:127
  5.6 15.2 %collective-permute-start.1 = (bf16[1024,128]{1,0:T(8,128)(2,1)}, bf16[1024,128]{1,0:T(8,128)(2,1)S(1)}, u32[]{:S(2)}, u32[]{:S(2)}) collective-permute-start(bf16[1024,128]{1,0:T(8,128)(2,1)} %first_ref.1), channel_id=1, source_target_pairs={{0,192},{64,128},{128,64},{192,0},{1,193},{65,129},{129,65},{193,1... | collective-permute-start | bytes 786440 | tf_op jit(solution)/shard_map/ppermute | solution.py:127
  8.6 12.1 %collective-permute-start = (bf16[1024,128]{1,0:T(8,128)(2,1)}, bf16[1024,128]{1,0:T(8,128)(2,1)S(1)}, u32[]{:S(2)}, u32[]{:S(2)}) collective-permute-start(bf16[1024,128]{1,0:T(8,128)(2,1)} %first_ref.1), channel_id=1, source_target_pairs={{0,64},{64,0},{128,192},{192,128},{1,65},{65,1},{129,193},{193,129... | collective-permute-start | bytes 786440 | tf_op jit(solution)/shard_map/ppermute | solution.py:127
  10.6 12.7 %collective-permute-start.5 = (bf16[1024,128]{1,0:T(8,128)(2,1)}, bf16[1024,128]{1,0:T(8,128)(2,1)S(1)}, u32[]{:S(2)}, u32[]{:S(2)}) collective-permute-start(bf16[1024,128]{1,0:T(8,128)(2,1)} %first_ref.1), channel_id=1, source_target_pairs={{0,256},{256,0},{1,257},{257,1},{2,258},{258,2},{3,259},{259,3},{4... | collective-permute-start | bytes 786440 | tf_op jit(solution)/shard_map/ppermute | solution.py:130
  17.6 1.0 %copy-start.1 = (bf16[1024,128]{1,0:T(8,128)(2,1)S(1)}, bf16[1024,128]{1,0:T(8,128)(2,1)}, u32[]{:S(2)}) copy-start(bf16[1024,128]{1,0:T(8,128)(2,1)} %first_ref.1) | copy-start | bytes 786436
  18.7 4.6 %copy-start.2 = (bf16[1024,128]{1,0:T(8,128)(2,1)S(1)}, bf16[1024,128]{1,0:T(8,128)(2,1)}, u32[]{:S(2)}) copy-start(bf16[1024,128]{1,0:T(8,128)(2,1)} %first_ref.1) | copy-start | bytes 786436
  18.7 4.6 %copy-start.4 = (f32[1024]{0:T(1024)S(1)}, f32[1024]{0:T(1024)}, u32[]{:S(2)}) copy-start(f32[1024]{0:T(1024)} %param.5) | copy-start | bytes 12292
  18.7 4.8 %collective-permute-start.4 = (bf16[2,1024,128]{2,1,0:T(8,128)(2,1)S(1)}, bf16[2,1024,128]{2,1,0:T(8,128)(2,1)S(1)}, u32[]{:S(2)}, u32[]{:S(2)}) collective-permute-start(bf16[2,1024,128]{2,1,0:T(8,128)(2,1)S(1)} %stack_one.1.refs_0_), channel_id=1, source_target_pairs={{0,32},{32,0},{1,33},{33,1},{2,34},{34,2},{3,35},{35,3},{4,36},{36... | collective-permute-start | bytes 1572872 | tf_op jit(solution)/shard_map/ppermute | solution.py:133
  20.8 3.9 %collective-permute-start.2 = (bf16[2,1024,128]{2,1,0:T(8,128)(2,1)S(1)}, bf16[2,1024,128]{2,1,0:T(8,128)(2,1)S(1)}, u32[]{:S(2)}, u32[]{:S(2)}) collective-permute-start(bf16[2,1024,128]{2,1,0:T(8,128)(2,1)S(1)} %stack_two.1.refs_1_), channel_id=1, source_target_pairs={{0,32},{32,0},{1,33},{33,1},{2,34},{34,2},{3,35},{35,3},{4,36},{36... | collective-permute-start | bytes 1572872 | tf_op jit(solution)/shard_map/ppermute | solution.py:135
  25.1 32.2 %copy-start = (bf16[2048,256]{1,0:T(8,128)(2,1)S(1)}, bf16[2048,256]{1,0:T(8,128)(2,1)}, u32[]{:S(2)}) copy-start(bf16[2048,256]{1,0:T(8,128)(2,1)} %eigvec_ref) | copy-start | bytes 3145732
  47.8 9.5 %copy-start.3 = (s32[2048]{0:T(1024)S(1)}, s32[2048]{0:T(1024)}, u32[]{:S(2)}) copy-start(s32[2048]{0:T(1024)} %param.7) | copy-start | bytes 24580
  47.8 17.9 %all-to-all-start.1 = ((f32[4,64,128]{2,1,0:T(8,128)}), f32[4,64,128]{2,1,0:T(8,128)S(1)}, u32[]{:S(2)}, u32[]{:S(2)}) async-start(f32[4,64,128]{2,1,0:T(8,128)} %sum_y.1), calls=%async_computation.1 | async-start | bytes 262144 | tf_op jit(solution)/shard_map/all_to_all | solution.py:158
  59.5 6.2 %collective-permute-start.6 = (f32[16,1024]{1,0:T(8,128)S(1)}, f32[16,1024]{1,0:T(8,128)S(1)}, u32[]{:S(2)}, u32[]{:S(2)}) collective-permute-start(f32[16,1024]{1,0:T(8,128)S(1)} %modes_away.1), channel_id=1, source_target_pairs={{0,256},{256,0},{1,257},{257,1},{2,258},{258,2},{3,259},{259,3},{4... | collective-permute-start | bytes 196616 | tf_op jit(solution)/shard_map/ppermute | solution.py:166
